TPU v7x, 512 devices: a whole 4x8x8 slice. The times are simulated.
512 devices in a mesh: dom: 128 (over y, z, core), row: 4 (over x).
Axes of the slice: x: 4, y: 8, z: 8, core: 2. Of those that a mesh axis runs over, the one named last changes fastest.
Arguments:
- features: bfloat16 [65536, 256], P(('dom', 'row')), may hold values from -6 to 6
- history: bfloat16 [65536, 256], P(('dom', 'row')), may hold values from -6 to 6
- inner_adj: bfloat16 [65536, 512], P(('dom', 'row')), as said below
- halo_tiles: bfloat16 [32768, 4096], P(('dom', 'row')), may hold values from -0.125 to 0.125
- tile_target: int32 [512, 1024], P(('dom', 'row')), may hold values from 0 to 1
- pair_counts: int32 [512, 512], P(('dom', 'row')), may hold values from 0 to 2
- send_blocks: int32 [512, 1024], P(('dom', 'row')), may hold values from 0 to 31
- weight1: bfloat16 [256, 256], replicated, may hold values from -0.375 to 0.375
- weight2: bfloat16 [256, 256], replicated, may hold values from -0.375 to 0.375
- out_cotangent: bfloat16 [65536, 256], P(('dom', 'row')), may hold values from -0.0234375 to 0.0234375
Outputs:
- fresh_history: bfloat16 [65536, 256], P(('dom', 'row'))
- layer_out: bfloat16 [65536, 256], P(('dom', 'row'))
- grad_w1: float32 [256, 256], replicated
- grad_w2: float32 [256, 256], replicated
Inputs may be any that keep to these rules, and one draw needn't show every extreme that they name: pair_counts[e, o] blocks of the 2 slots from owner o to requester e are used, the lowest slots first; some pair uses all 2. Each partition's 512 x 512 block of inner_adj is symmetric.
All inputs are finite; a program needn't handle non-finite values.
Results may differ from a plain program's by a relative error of at most 0.011.
Values may be sent and summed in bfloat16 or wider, within the bound.
A program may use at most 64 MiB of HBM per device.

v0:
```python
import jax
import jax.numpy as jnp
from jax import lax
from jax.sharding import PartitionSpec as P

RB = 4
CAP = 2


def silu_slope(value):
    sig = jax.nn.sigmoid(value)
    return sig * (1.0 + value * (1.0 - sig))


def expand_tiles(halo_tiles, targets, counts, node_rows):
    nblocks = targets.shape[0]
    slot_rows = halo_tiles.shape[1]
    block_rows = slot_rows // nblocks
    usable = jnp.arange(nblocks, dtype=jnp.int32) % CAP < jnp.repeat(counts, CAP)
    tile_ids = jnp.arange(node_rows // halo_tiles.shape[0], dtype=jnp.int32)
    select = ((targets[None, :] == tile_ids[:, None]) & usable[None, :]).astype(jnp.bfloat16)
    select_rows = jnp.repeat(select, block_rows, axis=1)
    return (select_rows[:, None, :] * halo_tiles[None, :, :]).reshape(node_rows, slot_rows)


def pick_blocks(source, send_blocks, n_dom, n_row):
    width = source.shape[1]
    blocked = source.reshape(-1, RB, width)
    picked = jnp.take(blocked, send_blocks[0], axis=0)
    return picked.reshape(n_dom, n_row, CAP * RB, width)


def inner_sum(values, inner_adj):
    return jnp.dot(
        inner_adj,
        lax.all_gather(values, "row", axis=0, tiled=True),
        preferred_element_type=jnp.float32,
    )


def per_device(
    features,
    history,
    inner_adj,
    halo_tiles,
    tile_target,
    pair_counts,
    send_blocks,
    weight1,
    weight2,
    out_cotangent,
):
    n_dom = lax.axis_size("dom")
    n_row = lax.axis_size("row")
    width = features.shape[1]
    expanded = expand_tiles(halo_tiles, tile_target[0], pair_counts[0], inner_adj.shape[0])
    feat_halo = lax.all_to_all(
        lax.all_to_all(
            pick_blocks(features, send_blocks, n_dom, n_row),
            "dom",
            split_axis=0,
            concat_axis=0,
            tiled=True,
        ),
        "row",
        split_axis=1,
        concat_axis=1,
        tiled=True,
    )
    feat_halo = feat_halo.reshape(-1, width)
    inner_first = inner_sum(features, inner_adj)
    mixed_first = (
        inner_first + jnp.dot(expanded, feat_halo, preferred_element_type=jnp.float32)
    ).astype(jnp.bfloat16)
    pre_first = jnp.dot(mixed_first, weight1, preferred_element_type=jnp.float32)
    fresh_history = jax.nn.silu(pre_first).astype(jnp.bfloat16)
    hist_halo = lax.all_to_all(
        lax.all_to_all(
            pick_blocks(history, send_blocks, n_dom, n_row),
            "dom",
            split_axis=0,
            concat_axis=0,
            tiled=True,
        ),
        "row",
        split_axis=1,
        concat_axis=1,
        tiled=True,
    )
    hist_halo = hist_halo.reshape(-1, width)
    inner_second = inner_sum(fresh_history, inner_adj)
    mixed_second = (
        inner_second + jnp.dot(expanded, hist_halo, preferred_element_type=jnp.float32)
    ).astype(jnp.bfloat16)
    pre_second = jnp.dot(mixed_second, weight2, preferred_element_type=jnp.float32)
    layer_out = jax.nn.silu(pre_second).astype(jnp.bfloat16)
    back_second = (out_cotangent.astype(jnp.float32) * silu_slope(pre_second)).astype(jnp.bfloat16)
    local_second = lax.dot_general(
        mixed_second, back_second, (((0,), (0,)), ((), ())), preferred_element_type=jnp.float32
    )
    upstream = lax.dot_general(
        back_second, weight2, (((1,), (1,)), ((), ())), preferred_element_type=jnp.float32
    ).astype(jnp.bfloat16)
    spread = lax.psum_scatter(
        lax.dot_general(
            inner_adj, upstream, (((0,), (0,)), ((), ())), preferred_element_type=jnp.float32
        ),
        "row",
        scatter_dimension=0,
        tiled=True,
    )
    back_first = (spread * silu_slope(pre_first)).astype(jnp.bfloat16)
    local_first = lax.dot_general(
        mixed_first, back_first, (((0,), (0,)), ((), ())), preferred_element_type=jnp.float32
    )
    grad_one, grad_two = lax.psum((local_first, local_second), ("dom", "row"))
    return (fresh_history, layer_out, grad_one, grad_two)


def solution(mesh):
    in_specs = (
        P(("dom", "row"), None),
        P(("dom", "row"), None),
        P(("dom", "row"), None),
        P(("dom", "row"), None),
        P(("dom", "row"), None),
        P(("dom", "row"), None),
        P(("dom", "row"), None),
        P(),
        P(),
        P(("dom", "row"), None),
    )
    out_specs = (P(("dom", "row"), None), P(("dom", "row"), None), P(), P())
    return jax.shard_map(
        per_device, mesh=mesh, in_specs=in_specs, out_specs=out_specs, check_vma=False
    )
```

profile of v0, /device:TPU:1, one launch (start us, length us, event | category | flops | bytes accessed | tf_op | source)
XLA Modules:
  0.0 552.7 jit_solution(14029948368215542943)
XLA Ops:
  7.2 0.7 fusion.8
  7.9 0.7 compare_and_fusion
  8.6 0.9 reshape.68
  9.5 0.9 reshape.71
  10.3 4.0 gather_fusion
  14.3 8.5 %gather_fusion.1 = bf16[1024,4,256]{2,1,0:T(4,128)(2,1)} fusion(bf16[32,4,256]{2,1,0:T(4,128)(2,1)S(1)} %reshape.71, s32[1024]{0:T(1024)S(1)} %fusion.8), kind=kCustom, calls=%fused_computation.1.clone | custom fusion | bytes 4198400 | tf_op jit(solution)/shard_map/jit(_take)/gather | solution.py:29
  22.8 6.8 %broadcast_select_fusion = (bf16[1024,4,256]{2,1,0:T(4,128)(2,1)}, bf16[1024,4,256]{2,1,0:T(4,128)(2,1)}) fusion(bf16[1024,4,256]{2,1,0:T(4,128)(2,1)} %gather_fusion.1, pred[1024]{0:T(1024)(128)(4,1)S(1)} %compare_and_fusion, bf16[1024,4,256]{2,1,0:T(4,128)(2,1)S(1)} %gather_fusion), kind=kLoop, calls=%fused_computation.2 | loop fusion | flops 2097152 | bytes 8389632 | tf_op jit(solution)/shard_map/jit(_take)/select_n | solution.py:29
  29.7 4.0 reshape.69
  33.6 19.0 %all-to-all-start = ((bf16[128,4,8,256]{3,2,1,0:T(8,128)(2,1)}), bf16[128,4,8,256]{3,2,1,0:T(8,128)(2,1)}, u32[]{:S(2)}, u32[]{:S(2)}) async-start(bf16[128,4,8,256]{3,2,1,0:T(8,128)(2,1)} %reshape.69), calls=%async_computation | async-start | bytes 4194304 | tf_op jit(solution)/shard_map/all_to_all | solution.py:58
  52.7 2.1 reshape.72
  54.7 49.7 %all-to-all-done = bf16[128,4,8,256]{3,2,1,0:T(8,128)(2,1)} async-done(((bf16[128,4,8,256]{3,2,1,0:T(8,128)(2,1)}), bf16[128,4,8,256]{3,2,1,0:T(8,128)(2,1)}, u32[]{:S(2)}, u32[]{:S(2)}) %all-to-all-start) | async-done | bytes 2097184 | tf_op jit(solution)/shard_map/all_to_all | solution.py:58
  104.4 7.8 %all-to-all-start.2 = ((bf16[128,4,8,256]{3,2,1,0:T(8,128)(2,1)}), bf16[128,4,8,256]{3,2,1,0:T(8,128)(2,1)S(1)}, u32[]{:S(2)}, u32[]{:S(2)}) async-start(bf16[128,4,8,256]{3,2,1,0:T(8,128)(2,1)} %reshape.72), calls=%async_computation.2 | async-start | bytes 4194304 | tf_op jit(solution)/shard_map/all_to_all | solution.py:78
  112.2 3.1 copy.18
  115.3 49.1 %all-to-all-done.2 = bf16[128,4,8,256]{3,2,1,0:T(8,128)(2,1)S(1)} async-done(((bf16[128,4,8,256]{3,2,1,0:T(8,128)(2,1)}), bf16[128,4,8,256]{3,2,1,0:T(8,128)(2,1)S(1)}, u32[]{:S(2)}, u32[]{:S(2)}) %all-to-all-start.2) | async-done | bytes 2097184 | tf_op jit(solution)/shard_map/all_to_all | solution.py:78
  164.4 1.3 copy-done.2
  165.7 4.0 all-to-all-start.1
  170.4 0.8 mul.54
  171.2 28.5 %all_gather.6 = bf16[512,256]{1,0:T(8,128)(2,1)S(1)} all-gather(bf16[128,256]{1,0:T(8,128)(2,1)S(1)} %copy-done.3), channel_id=1, replica_groups=mesh['dom'=128,'row'=4] {'row'}, dimensions={0}, use_global_device_ids=true | all-gather | bytes 327680 | tf_op jit(solution)/shard_map/all_gather | solution.py:36
  199.7 3.0 copy.20
  202.7 4.5 all-to-all-start.3
  207.2 1.1 broadcast_multiply_fusion
  209.8 25.1 %all_gather.7 = bf16[512,256]{1,0:T(8,128)(2,1)S(1)} all-gather(bf16[128,256]{1,0:T(8,128)(2,1)S(1)} %get-tuple-element.13), channel_id=1, replica_groups=mesh['dom'=128,'row'=4] {'row'}, dimensions={0}, use_global_device_ids=true | all-gather | bytes 327680 | tf_op jit(solution)/shard_map/all_gather | solution.py:36
  234.9 1.9 copy.21
  236.8 1.0 fusion.12
  238.1 0.9 multiply_convert_fusion.2
  238.9 1.3 convolution_bitcast_fusion
  240.3 0.9 fusion.10
  241.2 24.2 %reduce-scatter.2.cloned.1.call-done = f32[128,256]{1,0:T(8,128)} async-done(((f32[512,256]{1,0:T(8,128)}), f32[128,256]{1,0:T(8,128)}) %reduce-scatter.2.cloned.1.call-update) | async-done | bytes 131088 | tf_op jit(solution)/shard_map/reduce_scatter | solution.py:104
  265.4 1.8 fusion.3
  267.3 275.3 %all-reduce.3.cloned.1.call-done = (f32[256,256]{1,0:T(8,128)}, f32[256,256]{1,0:T(8,128)}) async-done(((f32[256,256]{1,0:T(8,128)}, f32[256,256]{1,0:T(8,128)}), (f32[256,256]{1,0:T(8,128)}, f32[256,256]{1,0:T(8,128)})) %all-reduce.3.cloned.1.call-update) | async-done | bytes 524304 | tf_op jit(solution)/shard_map/psum | solution.py:116
  542.5 1.7 copy.28
  544.2 1.7 copy.29
  (35 shorter events, 2.4 us)
Async XLA Ops:
  7.2 202.0 %copy-start = (bf16[128,512]{1,0:T(8,128)(2,1)S(1)}, bf16[128,512]{1,0:T(8,128)(2,1)}, u32[]{:S(2)}) copy-start(bf16[128,512]{1,0:T(8,128)(2,1)} %param.14) | copy-start | bytes 393220
  33.6 19.0 %copy-start.1 = (bf16[1024,4,256]{2,1,0:T(4,128)(2,1)S(1)}, bf16[1024,4,256]{2,1,0:T(4,128)(2,1)}, u32[]{:S(2)}) copy-start(bf16[1024,4,256]{2,1,0:T(4,128)(2,1)} %get-tuple-element.7) | copy-start | bytes 6291460
  33.6 70.8 %all-to-all-start = ((bf16[128,4,8,256]{3,2,1,0:T(8,128)(2,1)}), bf16[128,4,8,256]{3,2,1,0:T(8,128)(2,1)}, u32[]{:S(2)}, u32[]{:S(2)}) async-start(bf16[128,4,8,256]{3,2,1,0:T(8,128)(2,1)} %reshape.69), calls=%async_computation | async-start | bytes 4194304 | tf_op jit(solution)/shard_map/all_to_all | solution.py:58
  104.4 59.9 %all-to-all-start.2 = ((bf16[128,4,8,256]{3,2,1,0:T(8,128)(2,1)}), bf16[128,4,8,256]{3,2,1,0:T(8,128)(2,1)S(1)}, u32[]{:S(2)}, u32[]{:S(2)}) async-start(bf16[128,4,8,256]{3,2,1,0:T(8,128)(2,1)} %reshape.72), calls=%async_computation.2 | async-start | bytes 4194304 | tf_op jit(solution)/shard_map/all_to_all | solution.py:78
  115.3 54.5 %copy-start.8 = (s32[1,512]{1,0:T(1,128)S(1)}, s32[1,512]{1,0:T(1,128)}, u32[]{:S(2)}) copy-start(s32[1,512]{1,0:T(1,128)} %param.17) | copy-start | bytes 6148
  115.3 54.8 %copy-start.7 = (s32[1,1024]{1,0:T(1,128)S(1)}, s32[1,1024]{1,0:T(1,128)}, u32[]{:S(2)}) copy-start(s32[1,1024]{1,0:T(1,128)} %param.16) | copy-start | bytes 12292
  115.3 55.9 %copy-start.3 = (bf16[128,256]{1,0:T(8,128)(2,1)S(1)}, bf16[128,256]{1,0:T(8,128)(2,1)}, u32[]{:S(2)}) copy-start(bf16[128,256]{1,0:T(8,128)(2,1)} %param.12) | copy-start | bytes 196612
  164.4 1.3 copy-start.2
  165.7 37.0 %all-to-all-start.1 = ((bf16[128,4,8,256]{3,2,0,1:T(8,128)(2,1)}), bf16[128,4,8,256]{3,2,0,1:T(8,128)(2,1)S(1)}, u32[]{:S(2)}, u32[]{:S(2)}) async-start(bf16[128,4,8,256]{3,2,0,1:T(8,128)(2,1)} %copy.18), calls=%async_computation.1 | async-start | bytes 4194304 | tf_op jit(solution)/shard_map/all_to_all | solution.py:57
  202.7 32.2 %all-to-all-start.3 = ((bf16[128,4,8,256]{3,2,0,1:T(8,128)(2,1)}), bf16[128,4,8,256]{3,2,0,1:T(8,128)(2,1)}, u32[]{:S(2)}, u32[]{:S(2)}) async-start(bf16[128,4,8,256]{3,2,0,1:T(8,128)(2,1)} %copy.20), calls=%async_computation.3 | async-start | bytes 4194304 | tf_op jit(solution)/shard_map/all_to_all | solution.py:77
  207.2 58.2 %reduce-scatter.2.cloned.1.call-start = ((), (), s32[]{:S(2)}) async-start(), calls=%async_computation.5 | async-start | bytes 655360 | tf_op jit(solution)/shard_map/reduce_scatter | solution.py:104
  208.7 0.9 copy-start.9
  209.8 27.0 %copy-start.5 = (bf16[128,256]{1,0:T(8,128)(2,1)}, bf16[128,256]{1,0:T(8,128)(2,1)S(1)}, u32[]{:S(2)}) copy-start(bf16[128,256]{1,0:T(8,128)(2,1)S(1)} %get-tuple-element.13) | copy-start | bytes 196612
  236.8 1.3 copy-start.4
  236.8 2.1 copy-start.6
  240.2 302.3 %all-reduce.3.cloned.1.call-start = ((), (), s32[]{:S(2)}) async-start(), calls=%async_computation.6 | async-start | bytes 1048576 | tf_op jit(solution)/shard_map/psum | solution.py:116
Sparse Core Ops, SparseCore 0:
  240.3 25.0 reduce-scatter.1
  271.2 271.3 all-reduce.2
where the time goes:
time: 554 us; the launch traced here: 553 us
  waiting for transfers between devices  398 us (72%)
  blocking collectives  53.6 us (10%)
  starting transfers between devices  35.3 us (6%)
  local copies, waits for them, and re-layouts  34.8 us (6%)
  between operations  14.3 us (3%)
  other arithmetic  9.41 us (2%)
  matrix products  6.94 us (1%)
    psum x1, waiting for transfers between devices, per_device(): grad_one, grad_two = lax.psum((local_first, local_second), ('dom', 'row'))  275 us
    all_gather x2, blocking collectives, inner_sum(): lax.all_gather(values, 'row', axis=0, tiled=True)  53.6 us
    all_to_all x1, waiting for transfers between devices, per_device(): lax.all_to_all(pick_blocks(features, send_blocks, n_dom, n_row), 'dom', s...  49.7 us
    all_to_all x1, waiting for transfers between devices, per_device(): lax.all_to_all(pick_blocks(history, send_blocks, n_dom, n_row), 'dom', sp...  49.1 us
    reduce_scatter x1, waiting for transfers between devices, per_device(): lax.psum_scatter(lax.dot_general(inner_adj, upstream, (((0,), (0,)), ((),...  24.2 us
    all_to_all x1, starting transfers between devices, per_device(): lax.all_to_all(pick_blocks(features, send_blocks, n_dom, n_row), 'dom', s...  19 us
    gather x2, local copies, waits for them, and re-layouts, pick_blocks(): picked = jnp.take(blocked, send_blocks[0], axis=0)  12.5 us
  transfers between devices with their start and end apart: 6, of which 4 were waited for; matrix products, arithmetic and copies ran while one was open for 2% of the time, Pallas kernels for 0%

commit v1 on v0

v1 whole, which is shorter than its diff:
```python
import functools

import jax
import jax.numpy as jnp
from jax import lax
from jax.experimental import pallas as pl
from jax.experimental.pallas import tpu as pltpu
from jax.sharding import PartitionSpec as P

RB = 4
CAP = 2
NY = 8
NZ = 8
NC = 2
NX = 4
ROWS = 128
WIDTH = 256
MESH = pl.DeviceIdType.MESH


def sigmoid(value):
    return 1.0 / (1.0 + jnp.exp(-value))


def silu_slope(value):
    sig = sigmoid(value)
    return sig * (1.0 + value * (1.0 - sig))


def dot(left, right, dims=((1,), (0,))):
    return lax.dot_general(left, right, (dims, ((), ())), preferred_element_type=jnp.float32)


def expand_tiles(halo_tiles, targets, counts, node_rows):
    nblocks = targets.shape[0]
    slot_rows = halo_tiles.shape[1]
    block_rows = slot_rows // nblocks
    usable = jnp.arange(nblocks, dtype=jnp.int32) % CAP < jnp.repeat(counts, CAP)
    tile_ids = jnp.arange(node_rows // halo_tiles.shape[0], dtype=jnp.int32)
    select = ((targets[None, :] == tile_ids[:, None]) & usable[None, :]).astype(jnp.bfloat16)
    select_rows = jnp.repeat(select, block_rows, axis=1)
    return (select_rows[:, None, :] * halo_tiles[None, :, :]).reshape(node_rows, slot_rows)


def pick_blocks(source, send_blocks, n_dom, n_row):
    width = source.shape[1]
    blocked = source.reshape(-1, RB, width)
    picked = jnp.take(blocked, send_blocks[0], axis=0)
    return picked.reshape(n_dom, n_row, CAP * RB, width)


def position():
    dom = lax.axis_index("dom")
    return dom // (NZ * NC), (dom // NC) % NZ, dom % NC, lax.axis_index("row")


def device(y, z, c, x):
    return ((y * NZ + z) * NC + c, x)


class Links:
    def __init__(self, send, recv):
        self.send, self.recv, self.used = send, recv, 0

    def copy(self, src, dst, target):
        made = pltpu.make_async_remote_copy(
            src_ref=src,
            dst_ref=dst,
            send_sem=self.send.at[self.used],
            recv_sem=self.recv.at[self.used],
            device_id=target,
            device_id_type=MESH,
        )
        self.used += 1
        made.start()
        return made


def tail_kernel(
    feat, halo1, halo2, adj, w1, w2, cot,
    fresh_out, layer_out, grad1, grad2,
    rows, share, half, from_core, from_x, part_x, from_z, part_z, from_y, whole_z, whole_x, send, recv,
):
    y, z, c, x = position()
    links = Links(send, recv)
    peers = [device(y, z, c, (x + k) % NX) for k in range(1, NX)]
    peers += [device(y, (z + k) % NZ, c, x) for k in range(1, NZ)]
    peers += [device((y + k) % NY, z, c, x) for k in range(1, NY)]
    peers += [device(y, z, 1 - c, x)]
    barrier = pltpu.get_barrier_semaphore()
    for peer in peers:
        pl.semaphore_signal(barrier, inc=1, device_id=peer, device_id_type=MESH)
    pl.semaphore_wait(barrier, len(peers))
    x_peers, z_peers, y_peers, twin = peers[:3], peers[3:10], peers[10:17], peers[17]
    mine = pl.ds(pl.multiple_of(x * ROWS, ROWS), ROWS)

    def spread_rows(slot, value):
        rows[slot, mine, :] = value
        return [links.copy(rows.at[slot, mine, :], rows.at[slot, mine, :], peer) for peer in x_peers]

    def finish(copies):
        for copy in copies:
            copy.wait()

    copies = spread_rows(0, feat[...])
    finish(copies)
    mixed1 = (dot(adj[...], rows[0]) + halo1[...]).astype(jnp.bfloat16)
    pre1 = dot(mixed1, w1[...])
    fresh = (pre1 * sigmoid(pre1)).astype(jnp.bfloat16)
    fresh_out[...] = fresh
    copies = spread_rows(1, fresh)
    finish(copies)
    mixed2 = (dot(adj[...], rows[1]) + halo2[...]).astype(jnp.bfloat16)
    pre2 = dot(mixed2, w2[...])
    layer_out[...] = (pre2 * sigmoid(pre2)).astype(jnp.bfloat16)
    back2 = (cot[...].astype(jnp.float32) * silu_slope(pre2)).astype(jnp.bfloat16)
    upstream = dot(back2, w2[...], ((1,), (1,))).astype(jnp.bfloat16)
    copies = spread_rows(2, upstream)
    share[1] = dot(mixed2, back2, ((0,), (0,)))
    finish(copies)
    back1 = (dot(adj[...], rows[2]) * silu_slope(pre1)).astype(jnp.bfloat16)
    share[0] = dot(mixed1, back1, ((0,), (0,)))

    copy = links.copy(share.at[1 - c], from_core, twin)
    copy.wait()
    half[...] = share[c] + from_core[...]
    piece = WIDTH // NX
    copies = []
    for k in range(1, NX):
        start = pl.multiple_of(((x + k) % NX) * piece, piece)
        copies.append(links.copy(half.at[pl.ds(start, piece), :], from_x.at[k - 1], x_peers[k - 1]))
    finish(copies)
    total = half[pl.ds(pl.multiple_of(x * piece, piece), piece), :]
    for k in range(NX - 1):
        total += from_x[k]
    part_x[...] = total
    small = piece // NZ
    copies = []
    for k in range(1, NZ):
        start = pl.multiple_of(((z + k) % NZ) * small, small)
        copies.append(links.copy(part_x.at[pl.ds(start, small), :], from_z.at[k - 1], z_peers[k - 1]))
    finish(copies)
    total = part_x[pl.ds(pl.multiple_of(z * small, small), small), :]
    for k in range(NZ - 1):
        total += from_z[k]
    from_y[y] = total
    finish([links.copy(from_y.at[y], from_y.at[y], peer) for peer in y_peers])
    total = from_y[0]
    for k in range(1, NY):
        total += from_y[k]
    at_z = pl.ds(pl.multiple_of(z * small, small), small)
    whole_z[at_z, :] = total
    finish([links.copy(whole_z.at[at_z, :], whole_z.at[at_z, :], peer) for peer in z_peers])
    at_x = pl.ds(pl.multiple_of(x * piece, piece), piece)
    whole_x[c, at_x, :] = whole_z[...]
    finish([links.copy(whole_x.at[c, at_x, :], whole_x.at[c, at_x, :], peer) for peer in x_peers])
    finish([links.copy(whole_x.at[c], whole_x.at[c], twin)])
    grad1[...] = whole_x[0]
    grad2[...] = whole_x[1]


def run_tail(features, halo1, halo2, inner_adj, weight1, weight2, cot):
    f32, bf16 = jnp.float32, jnp.bfloat16
    piece, small = WIDTH // NX, WIDTH // NX // NZ
    n_copies = 3 * 3 + 1 + 3 + 7 + 7 + 7 + 3 + 1
    vmem = pl.BlockSpec(memory_space=pltpu.VMEM)
    return pl.pallas_call(
        tail_kernel,
        out_shape=(
            jax.ShapeDtypeStruct((ROWS, WIDTH), bf16),
            jax.ShapeDtypeStruct((ROWS, WIDTH), bf16),
            jax.ShapeDtypeStruct((WIDTH, WIDTH), f32),
            jax.ShapeDtypeStruct((WIDTH, WIDTH), f32),
        ),
        in_specs=[vmem] * 7,
        out_specs=(vmem,) * 4,
        scratch_shapes=[
            pltpu.VMEM((3, NX * ROWS, WIDTH), bf16),
            pltpu.VMEM((2, WIDTH, WIDTH), f32),
            pltpu.VMEM((WIDTH, WIDTH), f32),
            pltpu.VMEM((WIDTH, WIDTH), f32),
            pltpu.VMEM((NX - 1, piece, WIDTH), f32),
            pltpu.VMEM((piece, WIDTH), f32),
            pltpu.VMEM((NZ - 1, small, WIDTH), f32),
            pltpu.VMEM((small, WIDTH), f32),
            pltpu.VMEM((NY, small, WIDTH), f32),
            pltpu.VMEM((piece, WIDTH), f32),
            pltpu.VMEM((2, WIDTH, WIDTH), f32),
            pltpu.SemaphoreType.DMA((n_copies,)),
            pltpu.SemaphoreType.DMA((n_copies,)),
        ],
        compiler_params=pltpu.CompilerParams(
            collective_id=0, has_side_effects=True, vmem_limit_bytes=32 * 1024 * 1024
        ),
        name="tail",
    )(features, halo1, halo2, inner_adj, weight1, weight2, cot)


def per_device(
    features,
    history,
    inner_adj,
    halo_tiles,
    tile_target,
    pair_counts,
    send_blocks,
    weight1,
    weight2,
    out_cotangent,
):
    n_dom = lax.axis_size("dom")
    n_row = lax.axis_size("row")
    width = features.shape[1]
    expanded = expand_tiles(halo_tiles, tile_target[0], pair_counts[0], inner_adj.shape[0])

    def halo_sum(source):
        halo = lax.all_to_all(
            lax.all_to_all(
                pick_blocks(source, send_blocks, n_dom, n_row),
                "dom",
                split_axis=0,
                concat_axis=0,
                tiled=True,
            ),
            "row",
            split_axis=1,
            concat_axis=1,
            tiled=True,
        )
        return jnp.dot(expanded, halo.reshape(-1, width), preferred_element_type=jnp.float32)

    return run_tail(
        features, halo_sum(features), halo_sum(history), inner_adj, weight1, weight2, out_cotangent
    )


def solution(mesh):
    spread = P(("dom", "row"), None)
    in_specs = (spread,) * 7 + (P(), P(), spread)
    out_specs = (spread, spread, P(), P())
    return jax.shard_map(
        per_device, mesh=mesh, in_specs=in_specs, out_specs=out_specs, check_vma=False
    )
```

time: 554 us -> 276 us (0.50)
  waiting for transfers between devices: 398 us -> 142 us
  blocking collectives: 53.6 us -> 0 us
  Pallas kernels: 0 us -> 51.9 us
  between operations: 14.3 us -> 0.81 us
  matrix products: 6.94 us -> 0.97 us
    psum x1 -> x0, waiting for transfers between devices: 275 us -> none  [per_device(): grad_one, grad_two = lax.psum((local_first, local_second), ('dom', 'row'))]
    all_gather x2 -> x0, blocking collectives: 53.6 us -> none  [inner_sum(): lax.all_gather(values, 'row', axis=0, tiled=True)]
    pallas_call x0 -> x1, Pallas kernels: none -> 51.9 us  [run_tail(): pl.pallas_call(tail_kernel, out_shape=(jax.ShapeDtypeStruct((ROWS, WIDTH)...]
    all_to_all x4, waiting for transfers between devices: 98.8 us -> 142 us  [the longest x2 98.8 us: halo_sum(): lax.all_to_all(pick_blocks(source, send_blocks, n_dom, n_row), 'dom', spl...]
    reduce_scatter x1 -> x0, waiting for transfers between devices: 24.2 us -> none  [per_device(): lax.psum_scatter(lax.dot_general(inner_adj, upstream, (((0,), (0,)), ((),...]
    dot_general x9 -> x2, matrix products: 6.94 us -> 0.97 us  [halo_sum(): jnp.dot(expanded, halo.reshape(-1, width), preferred_element_type=jnp.flo...]
  transfers between devices with their start and end apart: 6 -> 4, of which waited for: 4 -> 4; matrix products, arithmetic and copies ran while one was open for 2% -> 4% of each run, Pallas kernels for 0% -> 0%
where the time goes in v1:
time: 276 us; the launch traced here: 275 us
  waiting for transfers between devices  142 us (51%)
  Pallas kernels  51.9 us (19%)
  starting transfers between devices  35.3 us (13%)
  local copies, waits for them, and re-layouts  34.6 us (13%)
  other arithmetic  9.39 us (3%)
    all_to_all x2, waiting for transfers between devices, halo_sum(): lax.all_to_all(pick_blocks(source, send_blocks, n_dom, n_row), 'dom', spl...  98.8 us
    pallas_call x1, Pallas kernels, run_tail(): pl.pallas_call(tail_kernel, out_shape=(jax.ShapeDtypeStruct((ROWS, WIDTH)...  51.9 us
    all_to_all x2, waiting for transfers between devices, halo_sum(): lax.all_to_all(lax.all_to_all(pick_blocks(source, send_blocks, n_dom, n_r...  43.5 us
    all_to_all x2, starting transfers between devices, halo_sum(): lax.all_to_all(pick_blocks(source, send_blocks, n_dom, n_row), 'dom', spl...  26.8 us
    gather x2, local copies, waits for them, and re-layouts, pick_blocks(): picked = jnp.take(blocked, send_blocks[0], axis=0)  12.5 us
    all_to_all x2, starting transfers between devices, halo_sum(): lax.all_to_all(lax.all_to_all(pick_blocks(source, send_blocks, n_dom, n_r...  8.49 us
    select_n x1, other arithmetic, pick_blocks(): picked = jnp.take(blocked, send_blocks[0], axis=0)  6.85 us
    all_to_all x2, local copies, waits for them, and re-layouts, halo_sum(): lax.all_to_all(pick_blocks(source, send_blocks, n_dom, n_row), 'dom', spl...  6.11 us
  transfers between devices with their start and end apart: 4, of which 4 were waited for; matrix products, arithmetic and copies ran while one was open for 4% of the time, Pallas kernels for 0%

profile of v1, /device:TPU:1, one launch (start us, length us, event | category | flops | bytes accessed | tf_op | source)
XLA Modules:
  0.0 275.3 jit_solution(11761244836128646017)
XLA Ops:
  0.6 0.7 fusion.4
  1.3 0.7 compare_and_fusion
  2.0 0.9 reshape.68
  2.9 0.9 reshape.71
  3.7 4.0 %gather_fusion = bf16[1024,4,256]{2,1,0:T(4,128)(2,1)S(1)} fusion(bf16[32,4,256]{2,1,0:T(4,128)(2,1)S(1)} %reshape.68, s32[1024]{0:T(1024)S(1)} %fusion.4), kind=kCustom, calls=%fused_computation.clone | custom fusion | bytes 4198400 | tf_op jit(solution)/shard_map/jit(_take)/gather | solution.py:48
  7.7 8.6 %gather_fusion.1 = bf16[1024,4,256]{2,1,0:T(4,128)(2,1)} fusion(bf16[32,4,256]{2,1,0:T(4,128)(2,1)S(1)} %reshape.71, s32[1024]{0:T(1024)S(1)} %fusion.4), kind=kCustom, calls=%fused_computation.1.clone | custom fusion | bytes 4198400 | tf_op jit(solution)/shard_map/jit(_take)/gather | solution.py:48
  16.3 6.8 %broadcast_select_fusion = (bf16[1024,4,256]{2,1,0:T(4,128)(2,1)}, bf16[1024,4,256]{2,1,0:T(4,128)(2,1)}) fusion(bf16[1024,4,256]{2,1,0:T(4,128)(2,1)} %gather_fusion.1, pred[1024]{0:T(1024)(128)(4,1)S(1)} %compare_and_fusion, bf16[1024,4,256]{2,1,0:T(4,128)(2,1)S(1)} %gather_fusion), kind=kLoop, calls=%fused_computation.2 | loop fusion | flops 2097152 | bytes 8389632 | tf_op jit(solution)/shard_map/jit(_take)/select_n | solution.py:48
  23.1 4.0 %reshape.72 = bf16[128,4,8,256]{3,2,1,0:T(8,128)(2,1)} reshape(bf16[1024,4,256]{2,1,0:T(4,128)(2,1)} %get-tuple-element.5) | data formatting | bytes 4194304 | tf_op jit(solution)/shard_map/reshape | solution.py:49
  27.1 19.0 %all-to-all-start.2 = ((bf16[128,4,8,256]{3,2,1,0:T(8,128)(2,1)}), bf16[128,4,8,256]{3,2,1,0:T(8,128)(2,1)}, u32[]{:S(2)}, u32[]{:S(2)}) async-start(bf16[128,4,8,256]{3,2,1,0:T(8,128)(2,1)} %reshape.72), calls=%async_computation.2 | async-start | bytes 4194304 | tf_op jit(solution)/shard_map/all_to_all | solution.py:218
  46.2 2.1 reshape.69
  48.2 49.7 %all-to-all-done.2 = bf16[128,4,8,256]{3,2,1,0:T(8,128)(2,1)} async-done(((bf16[128,4,8,256]{3,2,1,0:T(8,128)(2,1)}), bf16[128,4,8,256]{3,2,1,0:T(8,128)(2,1)}, u32[]{:S(2)}, u32[]{:S(2)}) %all-to-all-start.2) | async-done | bytes 2097184 | tf_op jit(solution)/shard_map/all_to_all | solution.py:218
  97.9 7.8 %all-to-all-start = ((bf16[128,4,8,256]{3,2,1,0:T(8,128)(2,1)}), bf16[128,4,8,256]{3,2,1,0:T(8,128)(2,1)S(1)}, u32[]{:S(2)}, u32[]{:S(2)}) async-start(bf16[128,4,8,256]{3,2,1,0:T(8,128)(2,1)} %reshape.69), calls=%async_computation | async-start | bytes 4194304 | tf_op jit(solution)/shard_map/all_to_all | solution.py:218
  105.7 3.1 %copy.16 = bf16[128,4,8,256]{3,2,0,1:T(8,128)(2,1)} copy(bf16[128,4,8,256]{3,2,1,0:T(8,128)(2,1)} %all-to-all-done.2) | data formatting | bytes 4194304 | tf_op jit(solution)/shard_map/all_to_all | solution.py:218
  108.8 49.1 %all-to-all-done = bf16[128,4,8,256]{3,2,1,0:T(8,128)(2,1)S(1)} async-done(((bf16[128,4,8,256]{3,2,1,0:T(8,128)(2,1)}), bf16[128,4,8,256]{3,2,1,0:T(8,128)(2,1)S(1)}, u32[]{:S(2)}, u32[]{:S(2)}) %all-to-all-start) | async-done | bytes 2097184 | tf_op jit(solution)/shard_map/all_to_all | solution.py:218
  157.9 1.4 copy-done.6
  159.2 4.0 %all-to-all-start.3 = ((bf16[128,4,8,256]{3,2,0,1:T(8,128)(2,1)}), bf16[128,4,8,256]{3,2,0,1:T(8,128)(2,1)S(1)}, u32[]{:S(2)}, u32[]{:S(2)}) async-start(bf16[128,4,8,256]{3,2,0,1:T(8,128)(2,1)} %copy.16), calls=%async_computation.3 | async-start | bytes 4194304 | tf_op jit(solution)/shard_map/all_to_all | solution.py:217
  163.6 3.0 %copy.14 = bf16[128,4,8,256]{3,2,0,1:T(8,128)(2,1)} copy(bf16[128,4,8,256]{3,2,1,0:T(8,128)(2,1)} %copy-done.6) | data formatting | bytes 4194304 | tf_op jit(solution)/shard_map/all_to_all | solution.py:218
  166.6 22.1 %all-to-all-done.3 = bf16[128,4,8,256]{3,2,0,1:T(8,128)(2,1)S(1)} async-done(((bf16[128,4,8,256]{3,2,0,1:T(8,128)(2,1)}), bf16[128,4,8,256]{3,2,0,1:T(8,128)(2,1)S(1)}, u32[]{:S(2)}, u32[]{:S(2)}) %all-to-all-start.3) | async-done | bytes 2097184 | tf_op jit(solution)/shard_map/all_to_all | solution.py:217
  188.7 4.5 %all-to-all-start.1 = ((bf16[128,4,8,256]{3,2,0,1:T(8,128)(2,1)}), bf16[128,4,8,256]{3,2,0,1:T(8,128)(2,1)}, u32[]{:S(2)}, u32[]{:S(2)}) async-start(bf16[128,4,8,256]{3,2,0,1:T(8,128)(2,1)} %copy.14), calls=%async_computation.1 | async-start | bytes 4194304 | tf_op jit(solution)/shard_map/all_to_all | solution.py:217
  193.2 0.3 broadcast_in_dim.19
  193.6 0.8 mul.29
  194.4 1.1 broadcast_multiply_fusion
  195.8 0.5 fusion.6.halo2
  196.3 21.5 %all-to-all-done.1 = bf16[128,4,8,256]{3,2,0,1:T(8,128)(2,1)} async-done(((bf16[128,4,8,256]{3,2,0,1:T(8,128)(2,1)}), bf16[128,4,8,256]{3,2,0,1:T(8,128)(2,1)}, u32[]{:S(2)}, u32[]{:S(2)}) %all-to-all-start.1) | async-done | bytes 2097184 | tf_op jit(solution)/shard_map/all_to_all | solution.py:217
  217.7 1.9 copy.15
  219.7 0.5 fusion.5.halo1
  220.2 0.3 copy-done
  220.7 51.9 %tail.1 = (bf16[128,256]{1,0:T(8,128)(2,1)S(1)}, bf16[128,256]{1,0:T(8,128)(2,1)S(1)}, f32[256,256]{1,0:T(8,128)S(1)}, f32[256,256]{1,0:T(8,128)S(1)}) custom-call(bf16[128,256]{1,0:T(8,128)(2,1)S(1)} %copy-done, f32[128,256]{1,0:T(8,128)S(1)} %fusion.5.halo1, f32[128,256]{1,0:T(8,128)S(1)} %fusion.6.halo2, bf16[128,512]{1,0:T(8,128)(2,1)S(1)} %copy-done.1, ...), custom_call_target="tpu_custom_call" | custom-call | tf_op jit(solution)/shard_map/tail/pallas_call | solution.py:167
  272.6 0.6 copy.22
  273.3 0.6 copy.23
  273.9 0.7 copy.24
  274.6 0.7 copy.25
  (21 shorter events, 0.9 us)
Async XLA Ops:
  27.1 19.0 %copy-start.5 = (bf16[1024,4,256]{2,1,0:T(4,128)(2,1)S(1)}, bf16[1024,4,256]{2,1,0:T(4,128)(2,1)}, u32[]{:S(2)}) copy-start(bf16[1024,4,256]{2,1,0:T(4,128)(2,1)} %get-tuple-element.6) | copy-start | bytes 6291460
  27.1 70.8 %all-to-all-start.2 = ((bf16[128,4,8,256]{3,2,1,0:T(8,128)(2,1)}), bf16[128,4,8,256]{3,2,1,0:T(8,128)(2,1)}, u32[]{:S(2)}, u32[]{:S(2)}) async-start(bf16[128,4,8,256]{3,2,1,0:T(8,128)(2,1)} %reshape.72), calls=%async_computation.2 | async-start | bytes 4194304 | tf_op jit(solution)/shard_map/all_to_all | solution.py:218
  97.9 59.9 %all-to-all-start = ((bf16[128,4,8,256]{3,2,1,0:T(8,128)(2,1)}), bf16[128,4,8,256]{3,2,1,0:T(8,128)(2,1)S(1)}, u32[]{:S(2)}, u32[]{:S(2)}) async-start(bf16[128,4,8,256]{3,2,1,0:T(8,128)(2,1)} %reshape.69), calls=%async_computation | async-start | bytes 4194304 | tf_op jit(solution)/shard_map/all_to_all | solution.py:218
  108.8 54.5 %copy-start.8 = (s32[1,512]{1,0:T(1,128)S(1)}, s32[1,512]{1,0:T(1,128)}, u32[]{:S(2)}) copy-start(s32[1,512]{1,0:T(1,128)} %param.17) | copy-start | bytes 6148
  157.9 1.4 copy-start.6
  159.2 29.5 %all-to-all-start.3 = ((bf16[128,4,8,256]{3,2,0,1:T(8,128)(2,1)}), bf16[128,4,8,256]{3,2,0,1:T(8,128)(2,1)S(1)}, u32[]{:S(2)}, u32[]{:S(2)}) async-start(bf16[128,4,8,256]{3,2,0,1:T(8,128)(2,1)} %copy.16), calls=%async_computation.3 | async-start | bytes 4194304 | tf_op jit(solution)/shard_map/all_to_all | solution.py:217
  166.6 26.6 %copy-start.7 = (s32[1,1024]{1,0:T(1,128)S(1)}, s32[1,1024]{1,0:T(1,128)}, u32[]{:S(2)}) copy-start(s32[1,1024]{1,0:T(1,128)} %param.16) | copy-start | bytes 12292
  188.7 29.0 %all-to-all-start.1 = ((bf16[128,4,8,256]{3,2,0,1:T(8,128)(2,1)}), bf16[128,4,8,256]{3,2,0,1:T(8,128)(2,1)}, u32[]{:S(2)}, u32[]{:S(2)}) async-start(bf16[128,4,8,256]{3,2,0,1:T(8,128)(2,1)} %copy.14), calls=%async_computation.1 | async-start | bytes 4194304 | tf_op jit(solution)/shard_map/all_to_all | solution.py:217
  219.6 0.8 copy-start
  219.6 0.9 copy-start.1
  219.6 1.0 copy-start.2
  219.7 1.0 copy-start.3
  219.7 1.0 copy-start.4

commit v2 on v1

v2 whole, which is shorter than its diff:
```python
import functools

import jax
import jax.numpy as jnp
from jax import lax
from jax.experimental import pallas as pl
from jax.experimental.pallas import tpu as pltpu
from jax.sharding import PartitionSpec as P

RB = 4
CAP = 2
NY = 8
NZ = 8
NC = 2
NX = 4
ROWS = 128
TILE = 64
CODED = 80
FIRST = 64
FIRST_CUT = 32
LAST_CUT = 96
KEPT = NZ * NX * CAP * RB
WIDTH = 256
MESH = pl.DeviceIdType.MESH


def sigmoid(value):
    return 1.0 / (1.0 + jnp.exp(-value))


def silu_slope(value):
    sig = sigmoid(value)
    return sig * (1.0 + value * (1.0 - sig))


def dot(left, right, dims=((1,), (0,))):
    return lax.dot_general(left, right, (dims, ((), ())), preferred_element_type=jnp.float32)


def position():
    dom = lax.axis_index("dom")
    return dom // (NZ * NC), (dom // NC) % NZ, dom % NC, lax.axis_index("row")


def device(y, z, c, x):
    return ((y * NZ + z) * NC + c, x)


class Links:
    def __init__(self, send, recv):
        self.send, self.recv, self.used = send, recv, 0

    def copy(self, src, dst, target):
        made = pltpu.make_async_remote_copy(
            src_ref=src,
            dst_ref=dst,
            send_sem=self.send.at[self.used],
            recv_sem=self.recv.at[self.used],
            device_id=target,
            device_id_type=MESH,
        )
        self.used += 1
        made.start()
        return made


def iota(shape, dim):
    return lax.broadcasted_iota(jnp.int32, shape, dim)


def one_hot(found):
    return jnp.where(found, 1.0, 0.0).astype(jnp.bfloat16)


def kernel(
    feat, hist, adj, tiles, code, picks, w1, w2, cot,
    fresh_out, layer_out, grad1, grad2,
    held, sb, wanted, chosen, order, codes, edges, twin_edges, seen, blocks,
    for_twin, own_sum, of_twin, parts, got,
    rows, share, half, from_core, from_x, part_x, from_z, from_y, whole_z, whole_x, send, recv,
):
    y, z, c, x = position()
    links = Links(send, recv)
    x_peers = [device(y, z, c, (x + k) % NX) for k in range(1, NX)]
    z_peers = [device(y, (z + k) % NZ, c, x) for k in range(1, NZ)]
    y_peers = [device((y + k) % NY, z, c, x) for k in range(1, NY)]
    twin = device(y, z, 1 - c, x)
    x_up, x_down, z_up, z_down = x_peers[0], x_peers[-1], z_peers[0], z_peers[-1]
    sent = []

    def move(src, dst, target):
        made = links.copy(src, dst, target)
        sent.append(made)
        return made

    def push(ref, target):
        return move(ref, ref, target)

    def arrive(copies):
        for copy in copies:
            copy.wait_recv()

    held[0, z, x] = feat[...]
    held[1, z, x] = hist[...]
    sb[z, x] = picks[...]
    barrier = pltpu.get_barrier_semaphore()
    peers = x_peers + z_peers + y_peers + [twin]
    for peer in peers:
        pl.semaphore_signal(barrier, inc=1, device_id=peer, device_id_type=MESH)
    pl.semaphore_wait(barrier, len(peers))

    top = pl.ds(0, FIRST)
    low = pl.ds(FIRST, ROWS - FIRST)

    def gather(a):
        def both_z(step, ref_up, ref_down):
            return [push(ref_up, z_up), push(ref_down, z_down)]

        def top_z(step):
            up, down = held.at[a, (z + NZ - step + 1) % NZ], held.at[a, (z + step - 1) % NZ]
            if step < NZ // 2:
                return both_z(step, up.at[:, top], down.at[:, top])
            return both_z(step, up.at[pl.ds(0, NX // 2), top], down.at[pl.ds(NX // 2, NX // 2), top])

        def low_z(step):
            up, down = held.at[a, (z + NZ - step + 1) % NZ, x], held.at[a, (z + step - 1) % NZ, x]
            if step < NZ // 2:
                return both_z(step, up.at[low], down.at[low])
            return both_z(
                step, up.at[pl.ds(FIRST, LAST_CUT - FIRST)], down.at[pl.ds(LAST_CUT, ROWS - LAST_CUT)]
            )

        x_left, x_right = (x + NX - 1) % NX, (x + 1) % NX
        tx1 = [push(held.at[a, z, x, top], x_up), push(held.at[a, z, x, top], x_down)]
        lz1 = low_z(1)
        yield
        arrive(tx1)
        tx2 = [
            push(held.at[a, z, x_left, pl.ds(0, FIRST_CUT)], x_up),
            push(held.at[a, z, x_right, pl.ds(FIRST_CUT, FIRST - FIRST_CUT)], x_down),
        ]
        yield
        arrive(lz1)
        lz2 = low_z(2)
        yield
        arrive(tx2)
        tz1 = top_z(1)
        yield
        arrive(lz2)
        lz3 = low_z(3)
        yield
        arrive(lz3)
        lz4 = low_z(4)
        yield
        arrive(tz1)
        tz2 = top_z(2)
        yield
        arrive(lz4)
        lx1 = [push(held.at[a, :, x, low], x_up), push(held.at[a, :, x, low], x_down)]
        yield
        arrive(tz2)
        tz3 = top_z(3)
        yield
        arrive(lx1)
        lx2 = [
            push(held.at[a, :, x_left, pl.ds(FIRST, LAST_CUT - FIRST)], x_up),
            push(held.at[a, :, x_right, pl.ds(LAST_CUT, ROWS - LAST_CUT)], x_down),
        ]
        yield
        arrive(tz3)
        tz4 = top_z(4)
        yield
        arrive(lx2)
        yield
        arrive(tz4)
        yield

    first, second = gather(0), gather(1)

    next(first)
    sb_x = [push(sb.at[z, x], peer) for peer in x_peers]

    span = NZ * NC * NX * CAP * RB
    n = iota((span, span), 1)
    place = ((n >> 5) & 7) * 64 + (((n >> 8) + c) & 1) * 32 + (n & 31)
    order[...] = one_hot(iota((span, span), 0) == place)
    n = iota((ROWS, span), 1)
    block = ((n >> 5) & 7) * 16 + (((n >> 8) + c) & 1) * 8 + ((n & 31) >> 2)
    codes[...] = dot(code[...].astype(jnp.bfloat16), one_hot(iota((ROWS, span), 0) == block))

    def cut(k, carry):
        at = pl.ds(pl.multiple_of(k * span, span), span)
        values = dot(tiles[:, at], order[...]).astype(jnp.bfloat16)
        marks = jnp.broadcast_to(codes[pl.ds(k, 1), :], (CODED - TILE, span)).astype(jnp.bfloat16)
        edges[c, k, 0:TILE, :] = values[:, :KEPT]
        edges[c, k, TILE:CODED, :] = marks[:, :KEPT]
        twin_edges[k, 0:TILE, :] = values[:, KEPT:]
        twin_edges[k, TILE:CODED, :] = marks[:, KEPT:]
        return carry

    next(first)
    lax.fori_loop(0, NY, cut, 0)
    across = move(twin_edges, edges.at[c], twin)
    arrive(sb_x)
    sb_z = [push(sb.at[z], peer) for peer in z_peers]
    next(first)
    next(first)
    arrive([across])
    seen[:, y] = edges[:, y]
    edge_copies = [
        move(edges.at[:, (y + k) % NY], seen.at[:, y], y_peers[k - 1]) for k in range(1, NY)
    ]
    next(first)
    next(first)
    next(second)

    arrive(sb_z)
    r = iota((ROWS, KEPT), 1)
    lane = ((z * NC + ((r >> 4) & 1)) * NX + x) * CAP + ((r >> 2) & 1)
    asked = dot(
        sb[...].reshape(NZ * NX * NY, ROWS).astype(jnp.bfloat16), one_hot(iota((ROWS, KEPT), 0) == lane)
    )
    i, r = iota((KEPT, KEPT), 0), iota((KEPT, KEPT), 1)
    fits = ((i & 7) == (r >> 5)) & (((i >> 3) & 1) == ((r >> 3) & 1))
    wanted[...] = jnp.where(fits, asked, 0.0).astype(jnp.bfloat16)

    def choose(q, carry):
        at = pl.ds(pl.multiple_of(q * 16, 16), 16)
        value = dot(wanted[at, :], jnp.ones((16, KEPT), jnp.bfloat16), ((0,), (0,)))
        r, lane = iota((KEPT, KEPT), 0), iota((KEPT, KEPT), 1)
        goal = lane - ((r >> 3) & 1) * ROWS - (r & 3)
        chosen[q] = one_hot(value * RB == goal.astype(jnp.float32))
        return carry

    lax.fori_loop(0, 16, choose, 0)
    for _ in range(5):
        next(first)
        next(second)
    next(first)
    next(first)
    next(second)

    def full_edges(core, k):
        values = seen[core, k, 0:TILE, :].astype(jnp.float32)
        mark = seen[core, k, TILE:CODED, :].astype(jnp.float32)[0:1, :]
        both = [jnp.where(mark == t, values, 0.0).astype(jnp.bfloat16) for t in range(ROWS // TILE)]
        return jnp.concatenate(both, axis=0)

    def partial_sums(a, between):
        def pick(q, carry):
            source = held[a, q // 2, pl.ds((q % 2) * 2, 2)].reshape(KEPT, WIDTH)
            value = dot(chosen[q], source).astype(jnp.bfloat16)
            blocks[:, pl.ds(pl.multiple_of(q * 16, 16), 16), :] = value.reshape(16, 16, WIDTH)
            return carry

        lax.fori_loop(0, 16, pick, 0)
        between()

        def twins(k, carry):
            value = dot(full_edges(1 - c, k), blocks[k * NC + 1 - c])
            for_twin[a, k] = value.astype(jnp.bfloat16)
            return carry

        lax.fori_loop(0, NY, twins, 0)
        crossing = move(for_twin.at[a], of_twin.at[a], twin)
        between()

        def own(k, carry):
            own_sum[k] = dot(full_edges(c, k), blocks[k * NC + c])
            return carry

        lax.fori_loop(0, NY, own, 0)
        between()
        arrive([crossing])
        copies = []
        for k in (4, 3, 5, 2, 6, 1, 7):
            to = (y + k) % NY
            parts[a, to] = (own_sum[to] + of_twin[a, to].astype(jnp.float32)).astype(jnp.bfloat16)
            copies.append(move(parts.at[a, to], got.at[a, y], y_peers[k - 1]))
        got[a, y] = (own_sum[y] + of_twin[a, y].astype(jnp.float32)).astype(jnp.bfloat16)
        return copies

    def halo_sum(a):
        total = got[a, 0].astype(jnp.float32)
        for k in range(1, NY):
            total += got[a, k].astype(jnp.float32)
        return total

    arrive(edge_copies)
    first_parts = partial_sums(0, lambda: next(second))
    for _ in second:
        pass
    second_parts = partial_sums(1, lambda: None)

    mine = pl.ds(pl.multiple_of(x * ROWS, ROWS), ROWS)

    def spread_rows(slot, value):
        rows[slot, mine, :] = value
        return [push(rows.at[slot, mine, :], peer) for peer in x_peers]

    inner1 = dot(adj[...], held[0, z].reshape(NX * ROWS, WIDTH))
    arrive(first_parts)
    mixed1 = (inner1 + halo_sum(0)).astype(jnp.bfloat16)
    pre1 = dot(mixed1, w1[...])
    fresh = (pre1 * sigmoid(pre1)).astype(jnp.bfloat16)
    fresh_out[...] = fresh
    copies = spread_rows(0, fresh)
    arrive(copies)
    inner2 = dot(adj[...], rows[0])
    arrive(second_parts)
    mixed2 = (inner2 + halo_sum(1)).astype(jnp.bfloat16)
    pre2 = dot(mixed2, w2[...])
    layer_out[...] = (pre2 * sigmoid(pre2)).astype(jnp.bfloat16)
    back2 = (cot[...].astype(jnp.float32) * silu_slope(pre2)).astype(jnp.bfloat16)
    upstream = dot(back2, w2[...], ((1,), (1,))).astype(jnp.bfloat16)
    copies = spread_rows(1, upstream)
    share[1] = dot(mixed2, back2, ((0,), (0,)))
    arrive(copies)
    back1 = (dot(adj[...], rows[1]) * silu_slope(pre1)).astype(jnp.bfloat16)
    share[0] = dot(mixed1, back1, ((0,), (0,)))

    arrive([move(share.at[1 - c], from_core, twin)])
    half[...] = share[c] + from_core[...]
    piece = WIDTH // NX
    copies = []
    for k in range(1, NX):
        start = pl.multiple_of(((x + k) % NX) * piece, piece)
        copies.append(move(half.at[pl.ds(start, piece), :], from_x.at[k - 1], x_peers[k - 1]))
    arrive(copies)
    total = half[pl.ds(pl.multiple_of(x * piece, piece), piece), :]
    for k in range(NX - 1):
        total += from_x[k]
    part_x[...] = total
    small = piece // NZ
    copies = []
    for k in range(1, NZ):
        start = pl.multiple_of(((z + k) % NZ) * small, small)
        copies.append(move(part_x.at[pl.ds(start, small), :], from_z.at[k - 1], z_peers[k - 1]))
    arrive(copies)
    total = part_x[pl.ds(pl.multiple_of(z * small, small), small), :]
    for k in range(NZ - 1):
        total += from_z[k]
    from_y[y] = total
    arrive([push(from_y.at[y], peer) for peer in y_peers])
    total = from_y[0]
    for k in range(1, NY):
        total += from_y[k]
    at_z = pl.ds(pl.multiple_of(z * small, small), small)
    whole_z[at_z, :] = total
    arrive([push(whole_z.at[at_z, :], peer) for peer in z_peers])
    at_x = pl.ds(pl.multiple_of(x * piece, piece), piece)
    whole_x[c, at_x, :] = whole_z[...]
    arrive([push(whole_x.at[c, at_x, :], peer) for peer in x_peers])
    arrive([push(whole_x.at[c], twin)])
    grad1[...] = whole_x[0]
    grad2[...] = whole_x[1]
    for copy in sent:
        copy.wait_send()


def per_device(
    features,
    history,
    inner_adj,
    halo_tiles,
    tile_target,
    pair_counts,
    send_blocks,
    weight1,
    weight2,
    out_cotangent,
):
    f32, bf16 = jnp.float32, jnp.bfloat16
    counts = jnp.repeat(pair_counts[0], CAP)
    usable = jnp.arange(counts.shape[0], dtype=jnp.int32) % CAP < counts
    code = jnp.where(usable, tile_target[0], -1).astype(f32).reshape(NY, ROWS)
    picks = send_blocks.astype(f32).reshape(NY, ROWS)
    piece, small = WIDTH // NX, WIDTH // NX // NZ
    span = NZ * NC * NX * CAP * RB
    n_copies = 200
    vmem = pl.BlockSpec(memory_space=pltpu.VMEM)
    return pl.pallas_call(
        kernel,
        out_shape=(
            jax.ShapeDtypeStruct((ROWS, WIDTH), bf16),
            jax.ShapeDtypeStruct((ROWS, WIDTH), bf16),
            jax.ShapeDtypeStruct((WIDTH, WIDTH), f32),
            jax.ShapeDtypeStruct((WIDTH, WIDTH), f32),
        ),
        in_specs=[vmem] * 9,
        out_specs=(vmem,) * 4,
        scratch_shapes=[
            pltpu.VMEM((2, NZ, NX, ROWS, WIDTH), bf16),
            pltpu.VMEM((NZ, NX, NY, ROWS), f32),
            pltpu.VMEM((KEPT, KEPT), bf16),
            pltpu.VMEM((16, KEPT, KEPT), bf16),
            pltpu.VMEM((span, span), bf16),
            pltpu.VMEM((NY, span), f32),
            pltpu.VMEM((NC, NY, CODED, KEPT), bf16),
            pltpu.VMEM((NY, CODED, KEPT), bf16),
            pltpu.VMEM((NC, NY, CODED, KEPT), bf16),
            pltpu.VMEM((NY * NC, KEPT, WIDTH), bf16),
            pltpu.VMEM((2, NY, ROWS, WIDTH), bf16),
            pltpu.VMEM((NY, ROWS, WIDTH), f32),
            pltpu.VMEM((2, NY, ROWS, WIDTH), bf16),
            pltpu.VMEM((2, NY, ROWS, WIDTH), bf16),
            pltpu.VMEM((2, NY, ROWS, WIDTH), bf16),
            pltpu.VMEM((2, NX * ROWS, WIDTH), bf16),
            pltpu.VMEM((2, WIDTH, WIDTH), f32),
            pltpu.VMEM((WIDTH, WIDTH), f32),
            pltpu.VMEM((WIDTH, WIDTH), f32),
            pltpu.VMEM((NX - 1, piece, WIDTH), f32),
            pltpu.VMEM((piece, WIDTH), f32),
            pltpu.VMEM((NZ - 1, small, WIDTH), f32),
            pltpu.VMEM((NY, small, WIDTH), f32),
            pltpu.VMEM((piece, WIDTH), f32),
            pltpu.VMEM((2, WIDTH, WIDTH), f32),
            pltpu.SemaphoreType.DMA((n_copies,)),
            pltpu.SemaphoreType.DMA((n_copies,)),
        ],
        compiler_params=pltpu.CompilerParams(
            collective_id=0, has_side_effects=True, vmem_limit_bytes=48 * 1024 * 1024
        ),
        name="layers",
    )(features, history, inner_adj, halo_tiles, code, picks, weight1, weight2, out_cotangent)


def solution(mesh):
    spread = P(("dom", "row"), None)
    in_specs = (spread,) * 7 + (P(), P(), spread)
    out_specs = (spread, spread, P(), P())
    return jax.shard_map(
        per_device, mesh=mesh, in_specs=in_specs, out_specs=out_specs, check_vma=False
    )
```

time: 276 us -> 132 us (0.48)
  waiting for transfers between devices: 142 us -> 0 us
  Pallas kernels: 51.9 us -> 121 us
  starting transfers between devices: 35.3 us -> 0 us
  local copies, waits for them, and re-layouts: 34.6 us -> 8.85 us
  other arithmetic: 9.39 us -> 1.37 us
    all_to_all x4 -> x0, waiting for transfers between devices: 142 us -> none  [the longest x2 98.8 us: halo_sum(): lax.all_to_all(pick_blocks(source, send_blocks, n_dom, n_row), 'dom', spl...]
    pallas_call x1, Pallas kernels: 51.9 us -> 121 us  [per_device(): pl.pallas_call(kernel, out_shape=(jax.ShapeDtypeStruct((ROWS, WIDTH), bf1...]
    all_to_all x4 -> x0, starting transfers between devices: 35.3 us -> none  [the longest x2 26.8 us: halo_sum(): lax.all_to_all(pick_blocks(source, send_blocks, n_dom, n_row), 'dom', spl...]
    gather x2 -> x0, local copies, waits for them, and re-layouts: 12.5 us -> none  [pick_blocks(): picked = jnp.take(blocked, send_blocks[0], axis=0)]
    all_to_all x4 -> x0, local copies, waits for them, and re-layouts: 8.26 us -> none  [the longest x2 6.11 us: halo_sum(): lax.all_to_all(pick_blocks(source, send_blocks, n_dom, n_row), 'dom', spl...]
    reshape x5 -> x0, local copies, waits for them, and re-layouts: 7.97 us -> none  [the longest x2 6.08 us: pick_blocks(): return picked.reshape(n_dom, n_row, CAP * RB, width)]
    select_n x1 -> x0, other arithmetic: 6.85 us -> none  [pick_blocks(): picked = jnp.take(blocked, send_blocks[0], axis=0)]
    unnamed x22 -> x23, local copies, waits for them, and re-layouts: 4.59 us -> 8.62 us
  transfers between devices with their start and end apart: 4 -> 0, of which waited for: 4 -> 0; matrix products, arithmetic and copies ran while one was open for 4% -> 0% of each run, Pallas kernels for 0% -> 0%
where the time goes in v2:
time: 132 us
  Pallas kernels  121 us (92%)
  local copies, waits for them, and re-layouts  8.85 us (7%)
  other arithmetic  1.37 us (1%)
    pallas_call x1, Pallas kernels, per_device(): pl.pallas_call(kernel, out_shape=(jax.ShapeDtypeStruct((ROWS, WIDTH), bf1...  121 us
    unnamed x23, local copies, waits for them, and re-layouts  8.62 us

profile of v2, /device:TPU:1, one launch (start us, length us, event | category | flops | bytes accessed | tf_op | source)
XLA Modules:
  0.0 131.9 jit_solution(13999506947602076044)
XLA Ops:
  0.6 0.0 copy-start.8
  0.6 0.0 copy-start.1
  0.7 0.5 broadcast.19
  1.2 0.1 copy-done.8
  1.3 0.7 reduce.3
  2.0 0.1 broadcast_in_dim.11
  2.1 0.7 convert_element_type.8
  2.7 0.1 copy.14
  2.9 0.0 copy-start.4
  2.9 0.0 copy-start.7
  2.9 0.7 copy-done.7
  3.6 0.0 copy-done.1
  3.6 0.1 copy-done.4
  3.7 0.0 copy-start
  3.7 1.0 copy-done
  4.7 0.0 copy-start.2
  4.7 0.9 copy-done.2
  5.6 0.0 copy-start.3
  5.7 0.9 copy-done.3
  6.6 0.0 copy-start.5
  6.6 0.8 copy-done.5
  7.4 0.0 copy-start.6
  7.4 0.8 copy-done.6
  8.2 121.0 %layers.1 = (bf16[128,256]{1,0:T(8,128)(2,1)S(1)}, bf16[128,256]{1,0:T(8,128)(2,1)S(1)}, f32[256,256]{1,0:T(8,128)S(1)}, f32[256,256]{1,0:T(8,128)S(1)}) custom-call(bf16[128,256]{1,0:T(8,128)(2,1)S(1)} %copy-done.4, bf16[128,256]{1,0:T(8,128)(2,1)S(1)} %copy-done.5, bf16[128,512]{1,0:T(8,128)(2,1)S(1)} %copy-done.1, bf16[64,4096]{1,0:T(8,128)(2,1)S(1)} %copy-done, ...), custom_call_target="tpu_custom_call" | custom-call | tf_op jit(solution)/shard_map/layers/pallas_call | solution.py:382
  129.2 0.6 copy.20
  129.9 0.6 copy.21
  130.5 0.7 copy.22
  131.2 0.7 copy.23
  (3 shorter events, 0.1 us)
Async XLA Ops:
  0.6 0.7 copy-start.8
  0.6 3.0 %copy-start.1 = (bf16[128,512]{1,0:T(8,128)(2,1)S(1)}, bf16[128,512]{1,0:T(8,128)(2,1)}, u32[]{:S(2)}) copy-start(bf16[128,512]{1,0:T(8,128)(2,1)} %adj.1) | copy-start | bytes 393220
  2.9 0.8 copy-start.4
  2.9 0.7 copy-start.7
  3.7 1.0 copy-start
  4.7 0.9 copy-start.2
  5.6 0.9 copy-start.3
  6.6 0.8 copy-start.5
  7.4 0.8 copy-start.6

commit v3 on v2

v3 whole, which is shorter than its diff:
```python
import functools

import jax
import jax.numpy as jnp
from jax import lax
from jax.experimental import pallas as pl
from jax.experimental.pallas import tpu as pltpu
from jax.sharding import PartitionSpec as P

RB = 4
CAP = 2
NY = 8
NZ = 8
NC = 2
NX = 4
ROWS = 128
TILE = 64
CODED = 80
FIRST = 48
FIRST_CUT = 32
LAST_CUT = 96
NEAR_FAR = (4, 3, 5, 2, 6, 1, 7, 0)
KEPT = NZ * NX * CAP * RB
WIDTH = 256
MESH = pl.DeviceIdType.MESH


def sigmoid(value):
    return 1.0 / (1.0 + jnp.exp(-value))


def silu_slope(value):
    sig = sigmoid(value)
    return sig * (1.0 + value * (1.0 - sig))


def dot(left, right, dims=((1,), (0,))):
    return lax.dot_general(left, right, (dims, ((), ())), preferred_element_type=jnp.float32)


def position():
    dom = lax.axis_index("dom")
    return dom // (NZ * NC), (dom // NC) % NZ, dom % NC, lax.axis_index("row")


def device(y, z, c, x):
    return ((y * NZ + z) * NC + c, x)


class Links:
    def __init__(self, send, recv):
        self.send, self.recv, self.used = send, recv, 0

    def copy(self, src, dst, target):
        made = pltpu.make_async_remote_copy(
            src_ref=src,
            dst_ref=dst,
            send_sem=self.send.at[self.used],
            recv_sem=self.recv.at[self.used],
            device_id=target,
            device_id_type=MESH,
        )
        self.used += 1
        made.start()
        return made


def iota(shape, dim):
    return lax.broadcasted_iota(jnp.int32, shape, dim)


def one_hot(found):
    return jnp.where(found, 1.0, 0.0).astype(jnp.bfloat16)


def kernel(
    feat, hist, adj_in, tiles_in, target_in, counts_in, sends_in, w1_in, w2_in, cot_in,
    fresh_out, layer_out, grad1, grad2,
    adj, tiles, target, counts, sends, w1, w2, cot, layer,
    held, sb, code, used, wanted, chosen, order, codes, edges, twin_edges, seen, blocks,
    for_twin, of_twin, parts, got,
    rows, share, rounded, from_group, part, from_z, from_y, whole, final, grads, send, recv, near,
):
    y, z, c, x = position()
    links = Links(send, recv)
    x_peers = [device(y, z, c, (x + k) % NX) for k in range(1, NX)]
    z_peers = [device(y, (z + k) % NZ, c, x) for k in range(1, NZ)]
    y_peers = [device((y + k) % NY, z, c, x) for k in range(1, NY)]
    twin = device(y, z, 1 - c, x)
    across_peers = [device(y, z, 1 - c, (x + k) % NX) for k in range(1, NX)]
    x_up, x_down, z_up, z_down = x_peers[0], x_peers[-1], z_peers[0], z_peers[-1]
    sent = []
    local = []

    def move(src, dst, target):
        made = links.copy(src, dst, target)
        sent.append(made)
        return made

    def push(ref, target):
        return move(ref, ref, target)

    def arrive(copies):
        for copy in copies:
            copy.wait_recv()

    def here(src, dst):
        made = pltpu.make_async_copy(src, dst, near.at[len(local)])
        made.start()
        local.append(made)
        return made

    barrier = pltpu.get_barrier_semaphore()
    peers = x_peers + z_peers + y_peers + [twin] + across_peers
    for peer in peers:
        pl.semaphore_signal(barrier, inc=1, device_id=peer, device_id_type=MESH)
    load_feat = here(feat, held.at[0, z, x])
    load_sends = here(sends_in, sends)
    load_tiles = here(tiles_in, tiles)
    load_target = here(target_in, target)
    load_counts = here(counts_in, counts)
    load_hist = here(hist, held.at[1, z, x])
    later = [here(a, b) for a, b in ((adj_in, adj), (w1_in, w1), (w2_in, w2), (cot_in, cot))]

    top = pl.ds(0, FIRST)
    low = pl.ds(FIRST, ROWS - FIRST)
    low_first = pl.ds(FIRST, LAST_CUT - FIRST)
    low_last = pl.ds(LAST_CUT, ROWS - LAST_CUT)
    x_left, x_right = (x + NX - 1) % NX, (x + 1) % NX

    def gather(a):
        def top_z(step):
            up, down = held.at[a, (z + NZ - step + 1) % NZ], held.at[a, (z + step - 1) % NZ]
            if step < NZ // 2:
                return [push(up.at[:, top], z_up), push(down.at[:, top], z_down)]
            halves = pl.ds(0, NX // 2), pl.ds(NX // 2, NX // 2)
            return [push(up.at[halves[0], top], z_up), push(down.at[halves[1], top], z_down)]

        def low_z(step):
            up, down = held.at[a, (z + NZ - step + 1) % NZ, x], held.at[a, (z + step - 1) % NZ, x]
            if step < NZ // 2:
                return [push(up.at[low], z_up), push(down.at[low], z_down)]
            return [push(up.at[low_first], z_up), push(down.at[low_last], z_down)]

        def low_x(steps):
            made = []
            for k in steps:
                at = held.at[a, (z + k) % NZ, x, low]
                made += [push(at, x_up), push(at, x_down)]
            return made

        def low_x_on(steps):
            made = []
            for k in steps:
                at = held.at[a, (z + k) % NZ]
                made += [push(at.at[x_left, low_first], x_up), push(at.at[x_right, low_last], x_down)]
            return made

        lz1 = low_z(1)
        tx1 = [push(held.at[a, z, x, top], x_up), push(held.at[a, z, x, top], x_down)]
        lx1 = {0: low_x([0])}
        lx2 = []
        yield
        arrive(tx1)
        tx2 = [
            push(held.at[a, z, x_left, pl.ds(0, FIRST_CUT)], x_up),
            push(held.at[a, z, x_right, pl.ds(FIRST_CUT, FIRST - FIRST_CUT)], x_down),
        ]
        yield
        arrive(lz1)
        lz2 = low_z(2)
        lx1[1] = low_x([1, 7])
        yield
        arrive(tx2)
        tz1 = top_z(1)
        arrive(lx1[0])
        lx2 += low_x_on([0])
        yield
        arrive(lz2)
        lz3 = low_z(3)
        lx1[2] = low_x([2, 6])
        yield
        arrive(lx1[1])
        lx2 += low_x_on([1, 7])
        arrive(lz3)
        lz4 = low_z(4)
        lx1[3] = low_x([3, 5])
        yield
        arrive(tz1)
        tz2 = top_z(2)
        arrive(lx1[2])
        lx2 += low_x_on([2, 6])
        yield
        arrive(lz4)
        lx1[4] = low_x([4])
        yield
        arrive(tz2)
        tz3 = top_z(3)
        arrive(lx1[3])
        lx2 += low_x_on([3, 5])
        yield
        arrive(lx1[4])
        lx2 += low_x_on([4])
        yield
        arrive(tz3)
        tz4 = top_z(4)
        yield
        arrive(lx2)
        yield
        arrive(tz4)
        yield

    gathers = gather(0), gather(1)

    def step(which):
        for letter in which:
            next(gathers["FH".index(letter)])

    span = NZ * NC * NX * CAP * RB
    n = iota((span, span), 1)
    place = ((n >> 5) & 7) * 64 + (((n >> 8) + c) & 1) * 32 + (n & 31)
    order[...] = one_hot(iota((span, span), 0) == place)
    load_sends.wait()
    for k in range(NY):
        sb[z, x, k : k + 1, :] = sends[:, k * ROWS : (k + 1) * ROWS].astype(jnp.float32)

    pl.semaphore_wait(barrier, len(peers))
    load_feat.wait()
    step("F")
    sb_x = [push(sb.at[z, x], peer) for peer in x_peers]
    load_hist.wait()

    load_target.wait()
    load_counts.wait()
    for k in range(NY):
        code[k : k + 1, :] = target[:, k * ROWS : (k + 1) * ROWS].astype(jnp.float32)
        used[k : k + 1, :] = counts[:, k * TILE : (k + 1) * TILE].astype(jnp.float32)
    pairs = one_hot(iota((TILE, ROWS), 0) == (iota((TILE, ROWS), 1) >> 1))
    usable = (iota((NY, ROWS), 1) & 1).astype(jnp.float32) < dot(used[...].astype(jnp.bfloat16), pairs)
    marked = jnp.where(usable, code[...], -1.0).astype(jnp.bfloat16)
    n = iota((ROWS, span), 1)
    block = ((n >> 5) & 7) * 16 + (((n >> 8) + c) & 1) * 8 + ((n & 31) >> 2)
    codes[...] = dot(marked, one_hot(iota((ROWS, span), 0) == block))
    load_tiles.wait()

    def cut(k, carry):
        at = pl.ds(pl.multiple_of(k * span, span), span)
        values = dot(tiles[:, at], order[...]).astype(jnp.bfloat16)
        marks = jnp.broadcast_to(codes[pl.ds(k, 1), :], (CODED - TILE, span)).astype(jnp.bfloat16)
        edges[c, k, 0:TILE, :] = values[:, :KEPT]
        edges[c, k, TILE:CODED, :] = marks[:, :KEPT]
        twin_edges[k, 0:TILE, :] = values[:, KEPT:]
        twin_edges[k, TILE:CODED, :] = marks[:, KEPT:]
        return carry

    step("F")
    lax.fori_loop(0, NY // 2, cut, 0)
    step("F")
    lax.fori_loop(NY // 2, NY, cut, 0)
    across = move(twin_edges, edges.at[c], twin)
    step("FH")
    arrive(sb_x)
    sb_z = [push(sb.at[z], peer) for peer in z_peers]
    step("FHF")
    arrive([across])
    seen[:, y] = edges[:, y]
    edge_copies = [
        move(edges.at[:, (y + k) % NY], seen.at[:, y], y_peers[k - 1]) for k in range(1, NY)
    ]
    step("HF")

    arrive(sb_z)
    r = iota((ROWS, KEPT), 1)
    lane = ((z * NC + ((r >> 4) & 1)) * NX + x) * CAP + ((r >> 2) & 1)
    asked = dot(
        sb[...].reshape(NZ * NX * NY, ROWS).astype(jnp.bfloat16), one_hot(iota((ROWS, KEPT), 0) == lane)
    )
    i, r = iota((KEPT, KEPT), 0), iota((KEPT, KEPT), 1)
    fits = ((i & 7) == (r >> 5)) & (((i >> 3) & 1) == ((r >> 3) & 1))
    wanted[...] = jnp.where(fits, asked, 0.0).astype(jnp.bfloat16)

    def choose(q, carry):
        at = pl.ds(pl.multiple_of(q * 16, 16), 16)
        value = dot(wanted[at, :], jnp.ones((16, KEPT), jnp.bfloat16), ((0,), (0,)))
        r, lane = iota((KEPT, KEPT), 0), iota((KEPT, KEPT), 1)
        goal = lane - ((r >> 3) & 1) * ROWS - (r & 3)
        chosen[q] = one_hot(value * RB == goal.astype(jnp.float32))
        return carry

    lax.fori_loop(0, 8, choose, 0)
    step("HFH")
    lax.fori_loop(8, 16, choose, 0)
    step("FHFHFHFHF")

    def full_edges(core, k):
        values = seen[core, k, 0:TILE, :].astype(jnp.float32)
        mark = seen[core, k, TILE:CODED, :].astype(jnp.float32)[0:1, :]
        both = [jnp.where(mark == t, values, 0.0).astype(jnp.bfloat16) for t in range(ROWS // TILE)]
        return jnp.concatenate(both, axis=0)

    def partial_sums(a, between):
        def pick(q, carry):
            source = held[a, q // 2, pl.ds((q % 2) * 2, 2)].reshape(KEPT, WIDTH)
            value = dot(chosen[q], source).astype(jnp.bfloat16)
            blocks[:, pl.ds(pl.multiple_of(q * 16, 16), 16), :] = value.reshape(16, 16, WIDTH)
            return carry

        lax.fori_loop(0, 16, pick, 0)
        between()
        crossing = []
        for k in NEAR_FAR:
            to = (y + k) % NY
            for_twin[a, to] = dot(full_edges(1 - c, to), blocks[to * NC + 1 - c]).astype(jnp.bfloat16)
            crossing.append(move(for_twin.at[a, to], of_twin.at[a, to], twin))
        between()
        copies = []
        for k, copy in zip(NEAR_FAR, crossing):
            to = (y + k) % NY
            value = dot(full_edges(c, to), blocks[to * NC + c])
            arrive([copy])
            value = (value + of_twin[a, to].astype(jnp.float32)).astype(jnp.bfloat16)
            if k:
                parts[a, to] = value
                copies.append(move(parts.at[a, to], got.at[a, y], y_peers[k - 1]))
            else:
                got[a, y] = value
        return copies

    def halo_sum(a):
        total = got[a, 0].astype(jnp.float32)
        for k in range(1, NY):
            total += got[a, k].astype(jnp.float32)
        return total

    arrive(edge_copies)
    first_parts = partial_sums(0, lambda: step("H"))
    for _ in gathers[1]:
        pass
    second_parts = partial_sums(1, lambda: None)

    mine = pl.ds(pl.multiple_of(x * ROWS, ROWS), ROWS)

    def spread_rows(slot, value):
        rows[slot, mine, :] = value
        return [push(rows.at[slot, mine, :], peer) for peer in x_peers]

    for copy in later:
        copy.wait()
    inner1 = dot(adj[...], held[0, z].reshape(NX * ROWS, WIDTH))
    arrive(first_parts)
    mixed1 = (inner1 + halo_sum(0)).astype(jnp.bfloat16)
    pre1 = dot(mixed1, w1[...])
    copies = spread_rows(0, (pre1 * sigmoid(pre1)).astype(jnp.bfloat16))
    results = [here(rows.at[0, mine, :], fresh_out)]
    arrive(copies)
    inner2 = dot(adj[...], rows[0])
    arrive(second_parts)
    mixed2 = (inner2 + halo_sum(1)).astype(jnp.bfloat16)
    pre2 = dot(mixed2, w2[...])
    back2 = (cot[...].astype(jnp.float32) * silu_slope(pre2)).astype(jnp.bfloat16)
    upstream = dot(back2, w2[...], ((1,), (1,))).astype(jnp.bfloat16)
    copies = spread_rows(1, upstream)

    group = [(k, 0) for k in range(1, NX)] + [(k, 1) for k in range(NX)]
    group_peers = x_peers + [twin] + across_peers
    piece = WIDTH // len(group_peers + [0])
    own = pl.ds(pl.multiple_of((c * NX + x) * piece, piece), piece)

    def share_out(which, value):
        share[which] = value
        rounded[which] = value.astype(jnp.bfloat16)
        made = []
        for o, (k, flip) in enumerate(group):
            core = (c + flip) % NC
            at = pl.ds(pl.multiple_of((core * NX + (x + k) % NX) * piece, piece), piece)
            made.append(move(rounded.at[which, at, :], from_group.at[which, o], group_peers[o]))
        return made

    shares = share_out(1, dot(mixed2, back2, ((0,), (0,))))
    layer[...] = (pre2 * sigmoid(pre2)).astype(jnp.bfloat16)
    results.append(here(layer, layer_out))
    arrive(copies)
    back1 = (dot(adj[...], rows[1]) * silu_slope(pre1)).astype(jnp.bfloat16)
    shares += share_out(0, dot(mixed1, back1, ((0,), (0,))))
    arrive(shares)
    for which in range(2):
        total = share[which, own, :]
        for o in range(len(group)):
            total += from_group[which, o].astype(jnp.float32)
        part[which * piece : (which + 1) * piece, :] = total
    small = 2 * piece // NZ
    copies = []
    for k in range(1, NZ):
        start = pl.multiple_of(((z + k) % NZ) * small, small)
        copies.append(move(part.at[pl.ds(start, small), :], from_z.at[k - 1], z_peers[k - 1]))
    arrive(copies)
    at_z = pl.ds(pl.multiple_of(z * small, small), small)
    total = part[at_z, :]
    for k in range(NZ - 1):
        total += from_z[k]
    from_y[y] = total
    arrive([push(from_y.at[y], peer) for peer in y_peers])
    total = from_y[0]
    for k in range(1, NY):
        total += from_y[k]
    whole[at_z, :] = total
    arrive([push(whole.at[at_z, :], peer) for peer in z_peers])
    member = c * NX + x
    final[member] = whole[...].astype(jnp.bfloat16)
    arrive([push(final.at[member], peer) for peer in group_peers])
    for m in range(NC * NX):
        for which in range(2):
            piece_of = final[m, which * piece : (which + 1) * piece, :]
            grads[which, m * piece : (m + 1) * piece, :] = piece_of.astype(jnp.float32)
    results += [here(grads.at[0], grad1), here(grads.at[1], grad2)]
    for copy in sent:
        copy.wait_send()
    for copy in results:
        copy.wait()


def keep_kernel(*refs):
    count = (len(refs) - 2) // 3
    into, out = refs[-2:]
    loads = [pltpu.make_async_copy(refs[k], refs[2 * count + k], into.at[k]) for k in range(count)]
    stores = [pltpu.make_async_copy(refs[2 * count + k], refs[count + k], out.at[k]) for k in range(count)]
    for load in loads:
        load.start()
    for load, store in zip(loads, stores):
        load.wait()
        store.start()
    for store in stores:
        store.wait()


def per_device(*arguments):
    f32, bf16, i32 = jnp.float32, jnp.bfloat16, jnp.int32
    piece = WIDTH // (NX * NC)
    span = NZ * NC * NX * CAP * RB
    n_copies = 210
    anywhere = pl.BlockSpec(memory_space=pl.ANY)
    shapes = (
        jax.ShapeDtypeStruct((ROWS, WIDTH), bf16),
        jax.ShapeDtypeStruct((ROWS, WIDTH), bf16),
        jax.ShapeDtypeStruct((WIDTH, WIDTH), f32),
        jax.ShapeDtypeStruct((WIDTH, WIDTH), f32),
    )
    results = pl.pallas_call(
        kernel,
        out_shape=shapes,
        in_specs=[anywhere] * 10,
        out_specs=(anywhere,) * 4,
        scratch_shapes=[
            pltpu.VMEM((ROWS, NX * ROWS), bf16),
            pltpu.VMEM((TILE, NY * span), bf16),
            pltpu.VMEM((1, NY * ROWS), i32),
            pltpu.VMEM((1, NY * TILE), i32),
            pltpu.VMEM((1, NY * ROWS), i32),
            pltpu.VMEM((WIDTH, WIDTH), bf16),
            pltpu.VMEM((WIDTH, WIDTH), bf16),
            pltpu.VMEM((ROWS, WIDTH), bf16),
            pltpu.VMEM((ROWS, WIDTH), bf16),
            pltpu.VMEM((2, NZ, NX, ROWS, WIDTH), bf16),
            pltpu.VMEM((NZ, NX, NY, ROWS), f32),
            pltpu.VMEM((NY, ROWS), f32),
            pltpu.VMEM((NY, TILE), f32),
            pltpu.VMEM((KEPT, KEPT), bf16),
            pltpu.VMEM((16, KEPT, KEPT), bf16),
            pltpu.VMEM((span, span), bf16),
            pltpu.VMEM((NY, span), f32),
            pltpu.VMEM((NC, NY, CODED, KEPT), bf16),
            pltpu.VMEM((NY, CODED, KEPT), bf16),
            pltpu.VMEM((NC, NY, CODED, KEPT), bf16),
            pltpu.VMEM((NY * NC, KEPT, WIDTH), bf16),
            pltpu.VMEM((2, NY, ROWS, WIDTH), bf16),
            pltpu.VMEM((2, NY, ROWS, WIDTH), bf16),
            pltpu.VMEM((2, NY, ROWS, WIDTH), bf16),
            pltpu.VMEM((2, NY, ROWS, WIDTH), bf16),
            pltpu.VMEM((2, NX * ROWS, WIDTH), bf16),
            pltpu.VMEM((2, WIDTH, WIDTH), f32),
            pltpu.VMEM((2, WIDTH, WIDTH), bf16),
            pltpu.VMEM((2, NX * NC - 1, piece, WIDTH), bf16),
            pltpu.VMEM((2 * piece, WIDTH), f32),
            pltpu.VMEM((NZ - 1, 2 * piece // NZ, WIDTH), f32),
            pltpu.VMEM((NY, 2 * piece // NZ, WIDTH), f32),
            pltpu.VMEM((2 * piece, WIDTH), f32),
            pltpu.VMEM((NX * NC, 2 * piece, WIDTH), bf16),
            pltpu.VMEM((2, WIDTH, WIDTH), f32),
            pltpu.SemaphoreType.DMA((n_copies,)),
            pltpu.SemaphoreType.DMA((n_copies,)),
            pltpu.SemaphoreType.DMA((16,)),
        ],
        compiler_params=pltpu.CompilerParams(
            collective_id=0, has_side_effects=True, vmem_limit_bytes=56 * 1024 * 1024
        ),
        name="layers",
    )(*arguments)
    return pl.pallas_call(
        keep_kernel,
        out_shape=shapes,
        in_specs=[anywhere] * 4,
        out_specs=(anywhere,) * 4,
        scratch_shapes=[pltpu.VMEM(shape.shape, shape.dtype) for shape in shapes]
        + [pltpu.SemaphoreType.DMA((4,)), pltpu.SemaphoreType.DMA((4,))],
        compiler_params=pltpu.CompilerParams(vmem_limit_bytes=60 * 1024 * 1024),
        name="keep",
    )(*results)


def solution(mesh):
    spread = P(("dom", "row"), None)
    in_specs = (spread,) * 7 + (P(), P(), spread)
    out_specs = (spread, spread, P(), P())
    return jax.shard_map(
        per_device, mesh=mesh, in_specs=in_specs, out_specs=out_specs, check_vma=False
    )
```

time: 132 us -> 111 us (0.84)
  Pallas kernels: 121 us -> 110 us
  local copies, waits for them, and re-layouts: 8.85 us -> 0 us
  other arithmetic: 1.37 us -> 0 us
    pallas_call x1 -> x2, Pallas kernels: 121 us -> 110 us  [the longest x1 108 us: per_device(): pl.pallas_call(kernel, out_shape=shapes, in_specs=[anywhere] * 10, out_sp...]
    unnamed x23 -> x0, local copies, waits for them, and re-layouts: 8.62 us -> none
where the time goes in v3:
time: 111 us
  Pallas kernels  110 us (99%)
    pallas_call x1, Pallas kernels, per_device(): pl.pallas_call(kernel, out_shape=shapes, in_specs=[anywhere] * 10, out_sp...  108 us

profile of v3, /device:TPU:1, one launch (start us, length us, event | category | flops | bytes accessed | tf_op | source)
XLA Modules:
  0.0 110.8 jit_solution(9337572115150618333)
XLA Ops:
  0.6 108.3 %layers.1 = (bf16[128,256]{1,0:T(8,128)(2,1)}, bf16[128,256]{1,0:T(8,128)(2,1)}, f32[256,256]{1,0:T(8,128)}, f32[256,256]{1,0:T(8,128)}) custom-call(bf16[128,256]{1,0:T(8,128)(2,1)} %feat.1, bf16[128,256]{1,0:T(8,128)(2,1)} %hist.1, bf16[128,512]{1,0:T(8,128)(2,1)} %adj_in.1, bf16[64,4096]{1,0:T(8,128)(2,1)} %tiles_in.1, s32[1,1024]{1,0:T(1,128)} %target_in.1, ...), custom_call_target="tpu_custom_call" | custom-call | tf_op jit(solution)/shard_map/layers/pallas_call | solution.py:448
  108.9 1.9 %keep.1 = (bf16[128,256]{1,0:T(8,128)(2,1)}, bf16[128,256]{1,0:T(8,128)(2,1)}, f32[256,256]{1,0:T(8,128)}, f32[256,256]{1,0:T(8,128)}) custom-call(bf16[128,256]{1,0:T(8,128)(2,1)} %get-tuple-element.8.refs_0_, bf16[128,256]{1,0:T(8,128)(2,1)} %get-tuple-element.9.refs_1_, f32[256,256]{1,0:T(8,128)} %get-tuple-element.10.refs_2_, ...), custom_call_target="tpu_custom_call" | custom-call | tf_op jit(solution)/shard_map/keep/pallas_call | solution.py:498

commit v4 on v3

--- a/solution.py
+++ b/solution.py
@@ -16,10 +16,10 @@
 ROWS = 128
 TILE = 64
 CODED = 80
-FIRST = 48
-FIRST_CUT = 32
-LAST_CUT = 96
-NEAR_FAR = (4, 3, 5, 2, 6, 1, 7, 0)
+FIRST = 32
+LAST_CUT = 80
+HALF = ROWS // 2
+ORDER = (4, 3, 5, 1, 7, 2, 6, 0)
 KEPT = NZ * NX * CAP * RB
 WIDTH = 256
 MESH = pl.DeviceIdType.MESH
@@ -77,8 +77,8 @@
     feat, hist, adj_in, tiles_in, target_in, counts_in, sends_in, w1_in, w2_in, cot_in,
     fresh_out, layer_out, grad1, grad2,
     adj, tiles, target, counts, sends, w1, w2, cot, layer,
-    held, sb, code, used, wanted, chosen, order, codes, edges, twin_edges, seen, blocks,
-    for_twin, of_twin, parts, got,
+    held, sb, code, used, chosen, codes, edges, twin_edges, seen, blocks,
+    for_twin, of_twin, parts, second_hop, relay3, relay4, got,
     rows, share, rounded, from_group, part, from_z, from_y, whole, final, grads, send, recv, near,
 ):
     y, z, c, x = position()
@@ -89,6 +89,7 @@
     twin = device(y, z, 1 - c, x)
     across_peers = [device(y, z, 1 - c, (x + k) % NX) for k in range(1, NX)]
     x_up, x_down, z_up, z_down = x_peers[0], x_peers[-1], z_peers[0], z_peers[-1]
+    y_up, y_down, y_up2, y_down2 = y_peers[0], y_peers[-1], y_peers[1], y_peers[-2]
     sent = []
     local = []
 
@@ -127,21 +128,10 @@
     low_first = pl.ds(FIRST, LAST_CUT - FIRST)
     low_last = pl.ds(LAST_CUT, ROWS - LAST_CUT)
     x_left, x_right = (x + NX - 1) % NX, (x + 1) % NX
+    z_up2, z_down2 = z_peers[1], z_peers[-2]
+    before2, after2 = (z + NZ - 2) % NZ, (z + 2) % NZ
 
     def gather(a):
-        def top_z(step):
-            up, down = held.at[a, (z + NZ - step + 1) % NZ], held.at[a, (z + step - 1) % NZ]
-            if step < NZ // 2:
-                return [push(up.at[:, top], z_up), push(down.at[:, top], z_down)]
-            halves = pl.ds(0, NX // 2), pl.ds(NX // 2, NX // 2)
-            return [push(up.at[halves[0], top], z_up), push(down.at[halves[1], top], z_down)]
-
-        def low_z(step):
-            up, down = held.at[a, (z + NZ - step + 1) % NZ, x], held.at[a, (z + step - 1) % NZ, x]
-            if step < NZ // 2:
-                return [push(up.at[low], z_up), push(down.at[low], z_down)]
-            return [push(up.at[low_first], z_up), push(down.at[low_last], z_down)]
-
         def low_x(steps):
             made = []
             for k in steps:
@@ -156,58 +146,50 @@
                 made += [push(at.at[x_left, low_first], x_up), push(at.at[x_right, low_last], x_down)]
             return made
 
-        lz1 = low_z(1)
-        tx1 = [push(held.at[a, z, x, top], x_up), push(held.at[a, z, x, top], x_down)]
-        lx1 = {0: low_x([0])}
-        lx2 = []
-        yield
-        arrive(tx1)
-        tx2 = [
-            push(held.at[a, z, x_left, pl.ds(0, FIRST_CUT)], x_up),
-            push(held.at[a, z, x_right, pl.ds(FIRST_CUT, FIRST - FIRST_CUT)], x_down),
+        at = held.at[a, z, x, low]
+        lz_far = [push(at, z_up2), push(at, z_down2)]
+        tx = [push(held.at[a, z, x, top], peer) for peer in x_peers]
+        lz_near = [push(at, z_up), push(at, z_down)]
+        lx = {0: low_x([0])}
+        ends = []
+        yield
+        arrive(tx)
+        at = held.at[a, z, :, top]
+        tz_far = [push(at, z_up2), push(at, z_down2)]
+        tz_near = [push(at, z_up), push(at, z_down)]
+        yield
+        arrive(lz_far)
+        up, down = held.at[a, before2, x], held.at[a, after2, x]
+        lz_on = [push(up.at[low_first], z_up2), push(down.at[low_last], z_down2)]
+        lz_on += [push(up.at[low], z_up), push(down.at[low], z_down)]
+        lx[2] = low_x([2, 6])
+        yield
+        arrive(lz_near)
+        lx[1] = low_x([1, 7])
+        arrive(lx[0])
+        ends += low_x_on([0])
+        yield
+        arrive(tz_far)
+        up, down = held.at[a, before2], held.at[a, after2]
+        tz_on = [
+            push(up.at[pl.ds(0, NX // 2), top], z_up2),
+            push(down.at[pl.ds(NX // 2, NX // 2), top], z_down2),
+            push(up.at[:, top], z_up),
+            push(down.at[:, top], z_down),
         ]
         yield
-        arrive(lz1)
-        lz2 = low_z(2)
-        lx1[1] = low_x([1, 7])
-        yield
-        arrive(tx2)
-        tz1 = top_z(1)
-        arrive(lx1[0])
-        lx2 += low_x_on([0])
-        yield
-        arrive(lz2)
-        lz3 = low_z(3)
-        lx1[2] = low_x([2, 6])
-        yield
-        arrive(lx1[1])
-        lx2 += low_x_on([1, 7])
-        arrive(lz3)
-        lz4 = low_z(4)
-        lx1[3] = low_x([3, 5])
-        yield
-        arrive(tz1)
-        tz2 = top_z(2)
-        arrive(lx1[2])
-        lx2 += low_x_on([2, 6])
-        yield
-        arrive(lz4)
-        lx1[4] = low_x([4])
-        yield
-        arrive(tz2)
-        tz3 = top_z(3)
-        arrive(lx1[3])
-        lx2 += low_x_on([3, 5])
-        yield
-        arrive(lx1[4])
-        lx2 += low_x_on([4])
-        yield
-        arrive(tz3)
-        tz4 = top_z(4)
-        yield
-        arrive(lx2)
-        yield
-        arrive(tz4)
+        arrive(lz_on)
+        lx[3] = low_x([3, 5, 4])
+        yield
+        arrive(lx[2])
+        ends += low_x_on([2, 6])
+        arrive(lx[1])
+        ends += low_x_on([1, 7])
+        yield
+        arrive(lx[3])
+        ends += low_x_on([3, 5, 4])
+        yield
+        arrive(tz_near + tz_on + ends)
         yield
 
     gathers = gather(0), gather(1)
@@ -217,80 +199,69 @@
             next(gathers["FH".index(letter)])
 
     span = NZ * NC * NX * CAP * RB
-    n = iota((span, span), 1)
+    n = iota((1, span), 1)
     place = ((n >> 5) & 7) * 64 + (((n >> 8) + c) & 1) * 32 + (n & 31)
-    order[...] = one_hot(iota((span, span), 0) == place)
+    order = one_hot(iota((span, span), 0) == place)
+    block = ((n >> 5) & 7) * 16 + (((n >> 8) + c) & 1) * 8 + ((n & 31) >> 2)
+    block_order = one_hot(iota((ROWS, span), 0) == block)
     load_sends.wait()
     for k in range(NY):
         sb[z, x, k : k + 1, :] = sends[:, k * ROWS : (k + 1) * ROWS].astype(jnp.float32)
-
-    pl.semaphore_wait(barrier, len(peers))
-    load_feat.wait()
-    step("F")
-    sb_x = [push(sb.at[z, x], peer) for peer in x_peers]
-    load_hist.wait()
-
     load_target.wait()
     load_counts.wait()
     for k in range(NY):
         code[k : k + 1, :] = target[:, k * ROWS : (k + 1) * ROWS].astype(jnp.float32)
         used[k : k + 1, :] = counts[:, k * TILE : (k + 1) * TILE].astype(jnp.float32)
-    pairs = one_hot(iota((TILE, ROWS), 0) == (iota((TILE, ROWS), 1) >> 1))
-    usable = (iota((NY, ROWS), 1) & 1).astype(jnp.float32) < dot(used[...].astype(jnp.bfloat16), pairs)
+    pairs = one_hot(iota((TILE, ROWS), 0) == (iota((1, ROWS), 1) >> 1))
+    usable = (iota((1, ROWS), 1) & 1).astype(jnp.float32) < dot(used[...].astype(jnp.bfloat16), pairs)
     marked = jnp.where(usable, code[...], -1.0).astype(jnp.bfloat16)
-    n = iota((ROWS, span), 1)
-    block = ((n >> 5) & 7) * 16 + (((n >> 8) + c) & 1) * 8 + ((n & 31) >> 2)
-    codes[...] = dot(marked, one_hot(iota((ROWS, span), 0) == block))
+    codes[...] = dot(marked, block_order)
     load_tiles.wait()
-
-    def cut(k, carry):
-        at = pl.ds(pl.multiple_of(k * span, span), span)
-        values = dot(tiles[:, at], order[...]).astype(jnp.bfloat16)
-        marks = jnp.broadcast_to(codes[pl.ds(k, 1), :], (CODED - TILE, span)).astype(jnp.bfloat16)
+    stacked = jnp.concatenate([tiles[:, k * span : (k + 1) * span] for k in range(NY)], axis=0)
+    placed = dot(stacked, order).astype(jnp.bfloat16)
+    for k in range(NY):
+        values = placed[k * TILE : (k + 1) * TILE]
+        marks = jnp.broadcast_to(codes[k : k + 1, :], (CODED - TILE, span)).astype(jnp.bfloat16)
         edges[c, k, 0:TILE, :] = values[:, :KEPT]
         edges[c, k, TILE:CODED, :] = marks[:, :KEPT]
         twin_edges[k, 0:TILE, :] = values[:, KEPT:]
         twin_edges[k, TILE:CODED, :] = marks[:, KEPT:]
-        return carry
-
+    load_feat.wait()
+    load_hist.wait()
+
+    pl.semaphore_wait(barrier, len(peers))
     step("F")
-    lax.fori_loop(0, NY // 2, cut, 0)
-    step("F")
-    lax.fori_loop(NY // 2, NY, cut, 0)
+    sb_x = [push(sb.at[z, x], peer) for peer in x_peers]
     across = move(twin_edges, edges.at[c], twin)
-    step("FH")
-    arrive(sb_x)
-    sb_z = [push(sb.at[z], peer) for peer in z_peers]
-    step("FHF")
     arrive([across])
     seen[:, y] = edges[:, y]
     edge_copies = [
         move(edges.at[:, (y + k) % NY], seen.at[:, y], y_peers[k - 1]) for k in range(1, NY)
     ]
-    step("HF")
+    step("FFF")
+    arrive(sb_x)
+    sb_z = [push(sb.at[z], peer) for peer in z_peers]
+    step("HFHF")
 
     arrive(sb_z)
-    r = iota((ROWS, KEPT), 1)
+    r = iota((1, KEPT), 1)
     lane = ((z * NC + ((r >> 4) & 1)) * NX + x) * CAP + ((r >> 2) & 1)
     asked = dot(
-        sb[...].reshape(NZ * NX * NY, ROWS).astype(jnp.bfloat16), one_hot(iota((ROWS, KEPT), 0) == lane)
+        one_hot(iota((ROWS, KEPT), 0) == lane),
+        sb[...].reshape(NZ * NX * NY, ROWS).astype(jnp.bfloat16),
+        ((0,), (1,)),
     )
-    i, r = iota((KEPT, KEPT), 0), iota((KEPT, KEPT), 1)
+    r, i = iota((KEPT, KEPT), 0), iota((KEPT, KEPT), 1)
     fits = ((i & 7) == (r >> 5)) & (((i >> 3) & 1) == ((r >> 3) & 1))
-    wanted[...] = jnp.where(fits, asked, 0.0).astype(jnp.bfloat16)
-
-    def choose(q, carry):
-        at = pl.ds(pl.multiple_of(q * 16, 16), 16)
-        value = dot(wanted[at, :], jnp.ones((16, KEPT), jnp.bfloat16), ((0,), (0,)))
-        r, lane = iota((KEPT, KEPT), 0), iota((KEPT, KEPT), 1)
-        goal = lane - ((r >> 3) & 1) * ROWS - (r & 3)
-        chosen[q] = one_hot(value * RB == goal.astype(jnp.float32))
-        return carry
-
-    lax.fori_loop(0, 8, choose, 0)
-    step("HFH")
-    lax.fori_loop(8, 16, choose, 0)
-    step("FHFHFHFHF")
+    wanted = jnp.where(fits, asked, 0.0).astype(jnp.bfloat16)
+    pair = one_hot((iota((KEPT, ROWS), 0) >> 4) == iota((KEPT, ROWS), 1))
+    r = iota((KEPT, 1), 0)
+    base = ((r >> 3) & 1) * ROWS + (r & 3)
+    slots = dot(wanted, pair) * RB + base.astype(jnp.float32)
+    lanes = iota((1, KEPT), 1).astype(jnp.float32)
+    for q in range(16):
+        chosen[q] = one_hot(slots[:, q : q + 1] == lanes)
+    step("HFHFHF")
 
     def full_edges(core, k):
         values = seen[core, k, 0:TILE, :].astype(jnp.float32)
@@ -305,38 +276,64 @@
             blocks[:, pl.ds(pl.multiple_of(q * 16, 16), 16), :] = value.reshape(16, 16, WIDTH)
             return carry
 
-        lax.fori_loop(0, 16, pick, 0)
+        lax.fori_loop(0, 16, pick, 0, unroll=4)
         between()
         crossing = []
-        for k in NEAR_FAR:
+        for k in ORDER:
             to = (y + k) % NY
             for_twin[a, to] = dot(full_edges(1 - c, to), blocks[to * NC + 1 - c]).astype(jnp.bfloat16)
             crossing.append(move(for_twin.at[a, to], of_twin.at[a, to], twin))
         between()
-        copies = []
-        for k, copy in zip(NEAR_FAR, crossing):
+        relayed, direct = [], []
+        for k, copy in zip(ORDER, crossing):
             to = (y + k) % NY
             value = dot(full_edges(c, to), blocks[to * NC + c])
             arrive([copy])
-            value = (value + of_twin[a, to].astype(jnp.float32)).astype(jnp.bfloat16)
-            if k:
-                parts[a, to] = value
-                copies.append(move(parts.at[a, to], got.at[a, y], y_peers[k - 1]))
+            value += of_twin[a, to].astype(jnp.float32)
+            if k == 0:
+                got[a, 0] = value.astype(jnp.bfloat16)
+                continue
+            if k == 2 or k == 6:
+                second_hop[a, k // 4] = value
+                continue
+            parts[a, k] = value.astype(jnp.bfloat16)
+            if k == 4:
+                for side, to_y in enumerate((y_up2, y_down2)):
+                    at = pl.ds(side * HALF, HALF)
+                    relayed.append(move(parts.at[a, k, at], relay4.at[a, side], to_y))
+            elif k == 3 or k == 5:
+                side = 0 if k == 3 else 1
+                relayed.append(move(parts.at[a, k], relay3.at[a, side], (y_up, y_down)[side]))
             else:
-                got[a, y] = value
-        return copies
+                side = 0 if k == 1 else 1
+                direct.append(move(parts.at[a, k], got.at[a, 1 + side], (y_up, y_down)[side]))
+
+        def relay():
+            arrive(relayed)
+            for side, to_y in enumerate((y_up2, y_down2)):
+                value = second_hop[a, side] + relay3[a, side].astype(jnp.float32)
+                far = relay4[a, side].astype(jnp.float32)
+                k = 2 if side == 0 else 6
+                for at, add in ((0, side == 0), (HALF, side == 1)):
+                    rows_of = value[at : at + HALF]
+                    parts[a, k, at : at + HALF, :] = (rows_of + far if add else rows_of).astype(jnp.bfloat16)
+                direct.append(move(parts.at[a, k], got.at[a, 3 + side], to_y))
+            return direct
+
+        return relay
 
     def halo_sum(a):
         total = got[a, 0].astype(jnp.float32)
-        for k in range(1, NY):
+        for k in range(1, 5):
             total += got[a, k].astype(jnp.float32)
         return total
 
     arrive(edge_copies)
-    first_parts = partial_sums(0, lambda: step("H"))
+    relay_first = partial_sums(0, lambda: step("H"))
     for _ in gathers[1]:
         pass
-    second_parts = partial_sums(1, lambda: None)
+    first_parts = relay_first()
+    relay_second = partial_sums(1, lambda: None)
 
     mine = pl.ds(pl.multiple_of(x * ROWS, ROWS), ROWS)
 
@@ -351,6 +348,7 @@
     mixed1 = (inner1 + halo_sum(0)).astype(jnp.bfloat16)
     pre1 = dot(mixed1, w1[...])
     copies = spread_rows(0, (pre1 * sigmoid(pre1)).astype(jnp.bfloat16))
+    second_parts = relay_second()
     results = [here(rows.at[0, mine, :], fresh_out)]
     arrive(copies)
     inner2 = dot(adj[...], rows[0])
@@ -464,9 +462,7 @@
             pltpu.VMEM((NZ, NX, NY, ROWS), f32),
             pltpu.VMEM((NY, ROWS), f32),
             pltpu.VMEM((NY, TILE), f32),
-            pltpu.VMEM((KEPT, KEPT), bf16),
             pltpu.VMEM((16, KEPT, KEPT), bf16),
-            pltpu.VMEM((span, span), bf16),
             pltpu.VMEM((NY, span), f32),
             pltpu.VMEM((NC, NY, CODED, KEPT), bf16),
             pltpu.VMEM((NY, CODED, KEPT), bf16),
@@ -475,7 +471,10 @@
             pltpu.VMEM((2, NY, ROWS, WIDTH), bf16),
             pltpu.VMEM((2, NY, ROWS, WIDTH), bf16),
             pltpu.VMEM((2, NY, ROWS, WIDTH), bf16),
-            pltpu.VMEM((2, NY, ROWS, WIDTH), bf16),
+            pltpu.VMEM((2, 2, ROWS, WIDTH), f32),
+            pltpu.VMEM((2, 2, ROWS, WIDTH), bf16),
+            pltpu.VMEM((2, 2, HALF, WIDTH), bf16),
+            pltpu.VMEM((2, 5, ROWS, WIDTH), bf16),
             pltpu.VMEM((2, NX * ROWS, WIDTH), bf16),
             pltpu.VMEM((2, WIDTH, WIDTH), f32),
             pltpu.VMEM((2, WIDTH, WIDTH), bf16),

time: 111 us -> 103 us (0.928)
  Pallas kernels: 110 us -> 102 us
    pallas_call x1, Pallas kernels: 108 us -> 100 us  [per_device(): pl.pallas_call(kernel, out_shape=shapes, in_specs=[anywhere] * 10, out_sp...]
where the time goes in v4:
time: 103 us
  Pallas kernels  102 us (99%)
    pallas_call x1, Pallas kernels, per_device(): pl.pallas_call(kernel, out_shape=shapes, in_specs=[anywhere] * 10, out_sp...  100 us

profile of v4, /device:TPU:1, one launch (start us, length us, event | category | flops | bytes accessed | tf_op | source)
XLA Modules:
  0.0 102.7 jit_solution(18270799507259266804)
XLA Ops:
  0.6 100.2 %layers.1 = (bf16[128,256]{1,0:T(8,128)(2,1)}, bf16[128,256]{1,0:T(8,128)(2,1)}, f32[256,256]{1,0:T(8,128)}, f32[256,256]{1,0:T(8,128)}) custom-call(bf16[128,256]{1,0:T(8,128)(2,1)} %feat.1, bf16[128,256]{1,0:T(8,128)(2,1)} %hist.1, bf16[128,512]{1,0:T(8,128)(2,1)} %adj_in.1, bf16[64,4096]{1,0:T(8,128)(2,1)} %tiles_in.1, s32[1,1024]{1,0:T(1,128)} %target_in.1, ...), custom_call_target="tpu_custom_call" | custom-call | tf_op jit(solution)/shard_map/layers/pallas_call | solution.py:446
  100.8 1.9 %keep.1 = (bf16[128,256]{1,0:T(8,128)(2,1)}, bf16[128,256]{1,0:T(8,128)(2,1)}, f32[256,256]{1,0:T(8,128)}, f32[256,256]{1,0:T(8,128)}) custom-call(bf16[128,256]{1,0:T(8,128)(2,1)} %get-tuple-element.8.refs_0_, bf16[128,256]{1,0:T(8,128)(2,1)} %get-tuple-element.9.refs_1_, f32[256,256]{1,0:T(8,128)} %get-tuple-element.10.refs_2_, ...), custom_call_target="tpu_custom_call" | custom-call | tf_op jit(solution)/shard_map/keep/pallas_call | solution.py:497

commit v5 on v4

--- a/solution.py
+++ b/solution.py
@@ -20,6 +20,7 @@
 LAST_CUT = 80
 HALF = ROWS // 2
 ORDER = (4, 3, 5, 1, 7, 2, 6, 0)
+FAR_FIRST = (4, 3, 5, 2, 6, 1, 7)
 KEPT = NZ * NX * CAP * RB
 WIDTH = 256
 MESH = pl.DeviceIdType.MESH
@@ -79,7 +80,7 @@
     adj, tiles, target, counts, sends, w1, w2, cot, layer,
     held, sb, code, used, chosen, codes, edges, twin_edges, seen, blocks,
     for_twin, of_twin, parts, second_hop, relay3, relay4, got,
-    rows, share, rounded, from_group, part, from_z, from_y, whole, final, grads, send, recv, near,
+    rows, slopes, turned, share, rounded, from_twin, halves, sending, from_row, leaving, arriving, part, from_z, from_y, whole, final, grads, send, recv, near,
 ):
     y, z, c, x = position()
     links = Links(send, recv)
@@ -87,7 +88,8 @@
     z_peers = [device(y, (z + k) % NZ, c, x) for k in range(1, NZ)]
     y_peers = [device((y + k) % NY, z, c, x) for k in range(1, NY)]
     twin = device(y, z, 1 - c, x)
-    across_peers = [device(y, z, 1 - c, (x + k) % NX) for k in range(1, NX)]
+    z_far_first = [z_peers[k - 1] for k in FAR_FIRST]
+    y_far_first = [y_peers[k - 1] for k in FAR_FIRST]
     x_up, x_down, z_up, z_down = x_peers[0], x_peers[-1], z_peers[0], z_peers[-1]
     y_up, y_down, y_up2, y_down2 = y_peers[0], y_peers[-1], y_peers[1], y_peers[-2]
     sent = []
@@ -112,7 +114,8 @@
         return made
 
     barrier = pltpu.get_barrier_semaphore()
-    peers = x_peers + z_peers + y_peers + [twin] + across_peers
+    peers = [peer for pair in zip(y_far_first, z_far_first) for peer in pair]
+    peers += x_peers + [twin]
     for peer in peers:
         pl.semaphore_signal(barrier, inc=1, device_id=peer, device_id_type=MESH)
     load_feat = here(feat, held.at[0, z, x])
@@ -121,7 +124,9 @@
     load_target = here(target_in, target)
     load_counts = here(counts_in, counts)
     load_hist = here(hist, held.at[1, z, x])
-    later = [here(a, b) for a, b in ((adj_in, adj), (w1_in, w1), (w2_in, w2), (cot_in, cot))]
+    mine = pl.ds(pl.multiple_of(x * ROWS, ROWS), ROWS)
+    adj_here = adj.at[mine, :]
+    later = [here(a, b) for a, b in ((adj_in, adj_here), (w1_in, w1), (w2_in, w2), (cot_in, cot))]
 
     top = pl.ds(0, FIRST)
     low = pl.ds(FIRST, ROWS - FIRST)
@@ -236,11 +241,11 @@
     arrive([across])
     seen[:, y] = edges[:, y]
     edge_copies = [
-        move(edges.at[:, (y + k) % NY], seen.at[:, y], y_peers[k - 1]) for k in range(1, NY)
+        move(edges.at[:, (y + k) % NY], seen.at[:, y], y_peers[k - 1]) for k in FAR_FIRST
     ]
     step("FFF")
     arrive(sb_x)
-    sb_z = [push(sb.at[z], peer) for peer in z_peers]
+    sb_z = [push(sb.at[z], peer) for peer in z_far_first]
     step("HFHF")
 
     arrive(sb_z)
@@ -332,26 +337,28 @@
     relay_first = partial_sums(0, lambda: step("H"))
     for _ in gathers[1]:
         pass
+    for copy in later:
+        copy.wait()
+    adj_copies = [push(adj_here, peer) for peer in x_peers]
     first_parts = relay_first()
     relay_second = partial_sums(1, lambda: None)
-
-    mine = pl.ds(pl.multiple_of(x * ROWS, ROWS), ROWS)
 
     def spread_rows(slot, value):
         rows[slot, mine, :] = value
         return [push(rows.at[slot, mine, :], peer) for peer in x_peers]
 
-    for copy in later:
-        copy.wait()
-    inner1 = dot(adj[...], held[0, z].reshape(NX * ROWS, WIDTH))
+    inner1 = dot(adj[mine, :], held[0, z].reshape(NX * ROWS, WIDTH))
     arrive(first_parts)
     mixed1 = (inner1 + halo_sum(0)).astype(jnp.bfloat16)
     pre1 = dot(mixed1, w1[...])
     copies = spread_rows(0, (pre1 * sigmoid(pre1)).astype(jnp.bfloat16))
     second_parts = relay_second()
     results = [here(rows.at[0, mine, :], fresh_out)]
+    slopes[x] = silu_slope(pre1).astype(jnp.bfloat16)
+    turned[x] = mixed1.T
     arrive(copies)
-    inner2 = dot(adj[...], rows[0])
+    row_copies = [push(ref.at[x], peer) for ref in (turned, slopes) for peer in x_peers]
+    inner2 = dot(adj[mine, :], rows[0])
     arrive(second_parts)
     mixed2 = (inner2 + halo_sum(1)).astype(jnp.bfloat16)
     pre2 = dot(mixed2, w2[...])
@@ -359,36 +366,53 @@
     upstream = dot(back2, w2[...], ((1,), (1,))).astype(jnp.bfloat16)
     copies = spread_rows(1, upstream)
 
-    group = [(k, 0) for k in range(1, NX)] + [(k, 1) for k in range(NX)]
-    group_peers = x_peers + [twin] + across_peers
-    piece = WIDTH // len(group_peers + [0])
-    own = pl.ds(pl.multiple_of((c * NX + x) * piece, piece), piece)
-
-    def share_out(which, value):
-        share[which] = value
-        rounded[which] = value.astype(jnp.bfloat16)
+    half = WIDTH // NC
+    piece = half // NX
+    kept = pl.ds(pl.multiple_of(c * half, half), half)
+    given = pl.ds(pl.multiple_of((1 - c) * half, half), half)
+
+    def to_row(crossing):
+        arrive([crossing])
+        value = share[kept, :] + from_twin[...].astype(jnp.float32)
+        halves[...] = value
+        sending[...] = value.astype(jnp.bfloat16)
         made = []
-        for o, (k, flip) in enumerate(group):
-            core = (c + flip) % NC
-            at = pl.ds(pl.multiple_of((core * NX + (x + k) % NX) * piece, piece), piece)
-            made.append(move(rounded.at[which, at, :], from_group.at[which, o], group_peers[o]))
+        for k in (2, 1, 3):
+            at = pl.ds(pl.multiple_of((x + k) % NX * piece, piece), piece)
+            made.append(move(sending.at[at, :], from_row.at[k - 1], x_peers[k - 1]))
         return made
 
-    shares = share_out(1, dot(mixed2, back2, ((0,), (0,))))
+    share[...] = dot(mixed2, back2, ((0,), (0,)))
+    rounded[...] = share[...].astype(jnp.bfloat16)
+    crossing = move(rounded.at[given, :], from_twin, twin)
     layer[...] = (pre2 * sigmoid(pre2)).astype(jnp.bfloat16)
     results.append(here(layer, layer_out))
+    shares = to_row(crossing)
+    arrive(shares)
+    own = pl.ds(pl.multiple_of(x * piece, piece), piece)
+    total = halves[own, :]
+    for k in range(NX - 1):
+        total += from_row[k].astype(jnp.float32)
+    part[piece : 2 * piece, :] = total
+
+    arrive(adj_copies)
+    arrive(row_copies)
     arrive(copies)
-    back1 = (dot(adj[...], rows[1]) * silu_slope(pre1)).astype(jnp.bfloat16)
-    shares += share_out(0, dot(mixed1, back1, ((0,), (0,))))
-    arrive(shares)
-    for which in range(2):
-        total = share[which, own, :]
-        for o in range(len(group)):
-            total += from_group[which, o].astype(jnp.float32)
-        part[which * piece : (which + 1) * piece, :] = total
+    spread = dot(adj[...], rows[1])
+    slope = slopes[...].reshape(NX * ROWS, WIDTH).astype(jnp.float32)
+    back1 = (spread * slope).astype(jnp.bfloat16)
+
+    def turned_rows(core):
+        at = pl.ds(pl.multiple_of(core * half + x * piece, piece), piece)
+        return jnp.concatenate([turned[k, at, :] for k in range(NX)], axis=1)
+
+    first_grad = dot(jnp.concatenate([turned_rows(1 - c), turned_rows(c)], axis=0), back1)
+    leaving[...] = first_grad[:piece].astype(jnp.bfloat16)
+    arrive([move(leaving, arriving, twin)])
+    part[0:piece, :] = first_grad[piece:] + arriving[...].astype(jnp.float32)
     small = 2 * piece // NZ
     copies = []
-    for k in range(1, NZ):
+    for k in FAR_FIRST:
         start = pl.multiple_of(((z + k) % NZ) * small, small)
         copies.append(move(part.at[pl.ds(start, small), :], from_z.at[k - 1], z_peers[k - 1]))
     arrive(copies)
@@ -397,19 +421,29 @@
     for k in range(NZ - 1):
         total += from_z[k]
     from_y[y] = total
-    arrive([push(from_y.at[y], peer) for peer in y_peers])
+    arrive([push(from_y.at[y], peer) for peer in y_far_first])
     total = from_y[0]
     for k in range(1, NY):
         total += from_y[k]
     whole[at_z, :] = total
-    arrive([push(whole.at[at_z, :], peer) for peer in z_peers])
-    member = c * NX + x
-    final[member] = whole[...].astype(jnp.bfloat16)
-    arrive([push(final.at[member], peer) for peer in group_peers])
-    for m in range(NC * NX):
-        for which in range(2):
-            piece_of = final[m, which * piece : (which + 1) * piece, :]
-            grads[which, m * piece : (m + 1) * piece, :] = piece_of.astype(jnp.float32)
+    arrive([push(whole.at[at_z, :], peer) for peer in z_far_first])
+    final[c, x] = whole[...].astype(jnp.bfloat16)
+    copies = [push(final.at[c, x], x_peers[k - 1]) for k in (2, 1, 3)]
+    crossings = [push(final.at[c, x], twin)]
+    for k, copy in zip((2, 1, 3), copies):
+        arrive([copy])
+        crossings.append(push(final.at[c, (x + NX - k) % NX], twin))
+
+    def unpack(core):
+        for m in range(NX):
+            for which in range(2):
+                at = pl.ds(pl.multiple_of(core * half + m * piece, piece), piece)
+                value = final[core, m, which * piece : (which + 1) * piece, :]
+                grads[which, at, :] = value.astype(jnp.float32)
+
+    unpack(c)
+    arrive(crossings)
+    unpack(1 - c)
     results += [here(grads.at[0], grad1), here(grads.at[1], grad2)]
     for copy in sent:
         copy.wait_send()
@@ -449,7 +483,7 @@
         in_specs=[anywhere] * 10,
         out_specs=(anywhere,) * 4,
         scratch_shapes=[
-            pltpu.VMEM((ROWS, NX * ROWS), bf16),
+            pltpu.VMEM((NX * ROWS, NX * ROWS), bf16),
             pltpu.VMEM((TILE, NY * span), bf16),
             pltpu.VMEM((1, NY * ROWS), i32),
             pltpu.VMEM((1, NY * TILE), i32),
@@ -476,14 +510,21 @@
             pltpu.VMEM((2, 2, HALF, WIDTH), bf16),
             pltpu.VMEM((2, 5, ROWS, WIDTH), bf16),
             pltpu.VMEM((2, NX * ROWS, WIDTH), bf16),
-            pltpu.VMEM((2, WIDTH, WIDTH), f32),
-            pltpu.VMEM((2, WIDTH, WIDTH), bf16),
-            pltpu.VMEM((2, NX * NC - 1, piece, WIDTH), bf16),
+            pltpu.VMEM((NX, ROWS, WIDTH), bf16),
+            pltpu.VMEM((NX, WIDTH, ROWS), bf16),
+            pltpu.VMEM((WIDTH, WIDTH), f32),
+            pltpu.VMEM((WIDTH, WIDTH), bf16),
+            pltpu.VMEM((WIDTH // NC, WIDTH), bf16),
+            pltpu.VMEM((WIDTH // NC, WIDTH), f32),
+            pltpu.VMEM((WIDTH // NC, WIDTH), bf16),
+            pltpu.VMEM((NX - 1, piece, WIDTH), bf16),
+            pltpu.VMEM((piece, WIDTH), bf16),
+            pltpu.VMEM((piece, WIDTH), bf16),
             pltpu.VMEM((2 * piece, WIDTH), f32),
             pltpu.VMEM((NZ - 1, 2 * piece // NZ, WIDTH), f32),
             pltpu.VMEM((NY, 2 * piece // NZ, WIDTH), f32),
             pltpu.VMEM((2 * piece, WIDTH), f32),
-            pltpu.VMEM((NX * NC, 2 * piece, WIDTH), bf16),
+            pltpu.VMEM((NC, NX, 2 * piece, WIDTH), bf16),
             pltpu.VMEM((2, WIDTH, WIDTH), f32),
             pltpu.SemaphoreType.DMA((n_copies,)),
             pltpu.SemaphoreType.DMA((n_copies,)),

time: 103 us -> 100 us (0.971)
  Pallas kernels: 102 us -> 99.3 us
    pallas_call x1, Pallas kernels: 100 us -> 97.4 us  [per_device(): pl.pallas_call(kernel, out_shape=shapes, in_specs=[anywhere] * 10, out_sp...]
where the time goes in v5:
time: 100 us; the launch traced here: 99.9 us
  Pallas kernels  99.3 us (99%)
    pallas_call x1, Pallas kernels, per_device(): pl.pallas_call(kernel, out_shape=shapes, in_specs=[anywhere] * 10, out_sp...  97.4 us

profile of v5, /device:TPU:1, one launch (start us, length us, event | category | flops | bytes accessed | tf_op | source)
XLA Modules:
  0.0 99.9 jit_solution(13766145913107222441)
XLA Ops:
  0.6 97.4 %layers.1 = (bf16[128,256]{1,0:T(8,128)(2,1)}, bf16[128,256]{1,0:T(8,128)(2,1)}, f32[256,256]{1,0:T(8,128)}, f32[256,256]{1,0:T(8,128)}) custom-call(bf16[128,256]{1,0:T(8,128)(2,1)} %feat.1, bf16[128,256]{1,0:T(8,128)(2,1)} %hist.1, bf16[128,512]{1,0:T(8,128)(2,1)} %adj_in.1, bf16[64,4096]{1,0:T(8,128)(2,1)} %tiles_in.1, s32[1,1024]{1,0:T(1,128)} %target_in.1, ...), custom_call_target="tpu_custom_call" | custom-call | tf_op jit(solution)/shard_map/layers/pallas_call | solution.py:480
  98.0 1.9 %keep.1 = (bf16[128,256]{1,0:T(8,128)(2,1)}, bf16[128,256]{1,0:T(8,128)(2,1)}, f32[256,256]{1,0:T(8,128)}, f32[256,256]{1,0:T(8,128)}) custom-call(bf16[128,256]{1,0:T(8,128)(2,1)} %get-tuple-element.8.refs_0_, bf16[128,256]{1,0:T(8,128)(2,1)} %get-tuple-element.9.refs_1_, f32[256,256]{1,0:T(8,128)} %get-tuple-element.10.refs_2_, ...), custom_call_target="tpu_custom_call" | custom-call | tf_op jit(solution)/shard_map/keep/pallas_call | solution.py:538

commit v6 on v5

--- a/solution.py
+++ b/solution.py
@@ -77,10 +77,10 @@
 def kernel(
     feat, hist, adj_in, tiles_in, target_in, counts_in, sends_in, w1_in, w2_in, cot_in,
     fresh_out, layer_out, grad1, grad2,
-    adj, tiles, target, counts, sends, w1, w2, cot, layer,
+    adj, tiles, target, counts, sends, w1, w2, w2_t, cot, layer,
     held, sb, code, used, chosen, codes, edges, twin_edges, seen, blocks,
     for_twin, of_twin, parts, second_hop, relay3, relay4, got,
-    rows, slopes, turned, share, rounded, from_twin, halves, sending, from_row, leaving, arriving, part, from_z, from_y, whole, final, grads, send, recv, near,
+    rows, slopes, turned, share, rounded, from_twin, halves, sending, from_row, leaving, arriving, part, folded, from_z, from_y, final, grads, send, recv, near,
 ):
     y, z, c, x = position()
     links = Links(send, recv)
@@ -106,6 +106,10 @@
     def arrive(copies):
         for copy in copies:
             copy.wait_recv()
+
+    def settle(leave):
+        while len(sent) > leave:
+            sent.pop(0).wait_send()
 
     def here(src, dst):
         made = pltpu.make_async_copy(src, dst, near.at[len(local)])
@@ -327,13 +331,18 @@
 
         return relay
 
-    def halo_sum(a):
-        total = got[a, 0].astype(jnp.float32)
-        for k in range(1, 5):
+    def near_sum(a, total, copies):
+        arrive(copies[:2])
+        for k in range(3):
             total += got[a, k].astype(jnp.float32)
         return total
 
+    def halo_sum(a, total, copies):
+        arrive(copies[2:])
+        return total + (got[a, 3].astype(jnp.float32) + got[a, 4].astype(jnp.float32))
+
     arrive(edge_copies)
+
     relay_first = partial_sums(0, lambda: step("H"))
     for _ in gathers[1]:
         pass
@@ -348,22 +357,24 @@
         return [push(rows.at[slot, mine, :], peer) for peer in x_peers]
 
     inner1 = dot(adj[mine, :], held[0, z].reshape(NX * ROWS, WIDTH))
-    arrive(first_parts)
-    mixed1 = (inner1 + halo_sum(0)).astype(jnp.bfloat16)
+    sum1 = near_sum(0, inner1, first_parts)
+    mixed1 = halo_sum(0, sum1, first_parts).astype(jnp.bfloat16)
     pre1 = dot(mixed1, w1[...])
     copies = spread_rows(0, (pre1 * sigmoid(pre1)).astype(jnp.bfloat16))
     second_parts = relay_second()
     results = [here(rows.at[0, mine, :], fresh_out)]
     slopes[x] = silu_slope(pre1).astype(jnp.bfloat16)
     turned[x] = mixed1.T
+    settle(40)
     arrive(copies)
     row_copies = [push(ref.at[x], peer) for ref in (turned, slopes) for peer in x_peers]
     inner2 = dot(adj[mine, :], rows[0])
-    arrive(second_parts)
-    mixed2 = (inner2 + halo_sum(1)).astype(jnp.bfloat16)
+    w2_t[...] = w2[...].T
+    sum2 = near_sum(1, inner2, second_parts)
+    mixed2 = halo_sum(1, sum2, second_parts).astype(jnp.bfloat16)
     pre2 = dot(mixed2, w2[...])
     back2 = (cot[...].astype(jnp.float32) * silu_slope(pre2)).astype(jnp.bfloat16)
-    upstream = dot(back2, w2[...], ((1,), (1,))).astype(jnp.bfloat16)
+    upstream = dot(back2, w2_t[...]).astype(jnp.bfloat16)
     copies = spread_rows(1, upstream)
 
     half = WIDTH // NC
@@ -388,6 +399,7 @@
     layer[...] = (pre2 * sigmoid(pre2)).astype(jnp.bfloat16)
     results.append(here(layer, layer_out))
     shares = to_row(crossing)
+    settle(8)
     arrive(shares)
     own = pl.ds(pl.multiple_of(x * piece, piece), piece)
     total = halves[own, :]
@@ -411,42 +423,53 @@
     arrive([move(leaving, arriving, twin)])
     part[0:piece, :] = first_grad[piece:] + arriving[...].astype(jnp.float32)
     small = 2 * piece // NZ
+    lanes = WIDTH // 2
+
+    def fold(value):
+        return jnp.concatenate([value[:, :lanes], value[:, lanes:]], axis=0).astype(jnp.bfloat16)
+
+    for k in range(NZ):
+        folded[k] = fold(part[k * small : (k + 1) * small, :])
     copies = []
     for k in FAR_FIRST:
-        start = pl.multiple_of(((z + k) % NZ) * small, small)
-        copies.append(move(part.at[pl.ds(start, small), :], from_z.at[k - 1], z_peers[k - 1]))
+        copies.append(move(folded.at[(z + k) % NZ], from_z.at[k - 1], z_peers[k - 1]))
+    settle(7)
     arrive(copies)
-    at_z = pl.ds(pl.multiple_of(z * small, small), small)
-    total = part[at_z, :]
+    total = folded[z].astype(jnp.float32)
     for k in range(NZ - 1):
-        total += from_z[k]
-    from_y[y] = total
-    arrive([push(from_y.at[y], peer) for peer in y_far_first])
-    total = from_y[0]
+        total += from_z[k].astype(jnp.float32)
+    from_y[y] = total.astype(jnp.bfloat16)
+    copies = [push(from_y.at[y], peer) for peer in y_far_first]
+    settle(7)
+    arrive(copies)
+    total = from_y[0].astype(jnp.float32)
     for k in range(1, NY):
-        total += from_y[k]
-    whole[at_z, :] = total
-    arrive([push(whole.at[at_z, :], peer) for peer in z_far_first])
-    final[c, x] = whole[...].astype(jnp.bfloat16)
+        total += from_y[k].astype(jnp.float32)
+    final[c, x, z] = total.astype(jnp.bfloat16)
+    copies = [push(final.at[c, x, z], peer) for peer in z_far_first]
+    settle(7)
+    arrive(copies)
     copies = [push(final.at[c, x], x_peers[k - 1]) for k in (2, 1, 3)]
     crossings = [push(final.at[c, x], twin)]
+    settle(4)
     for k, copy in zip((2, 1, 3), copies):
         arrive([copy])
         crossings.append(push(final.at[c, (x + NX - k) % NX], twin))
 
     def unpack(core):
         for m in range(NX):
-            for which in range(2):
-                at = pl.ds(pl.multiple_of(core * half + m * piece, piece), piece)
-                value = final[core, m, which * piece : (which + 1) * piece, :]
-                grads[which, at, :] = value.astype(jnp.float32)
+            for k in range(NZ):
+                which, row = divmod(k * small, piece)
+                at = pl.ds(pl.multiple_of(core * half + m * piece + row, small), small)
+                value = final[core, m, k].astype(jnp.float32)
+                grads[which, at, 0:lanes] = value[:small]
+                grads[which, at, lanes:WIDTH] = value[small:]
 
     unpack(c)
     arrive(crossings)
     unpack(1 - c)
     results += [here(grads.at[0], grad1), here(grads.at[1], grad2)]
-    for copy in sent:
-        copy.wait_send()
+    settle(0)
     for copy in results:
         copy.wait()
 
@@ -488,6 +511,7 @@
             pltpu.VMEM((1, NY * ROWS), i32),
             pltpu.VMEM((1, NY * TILE), i32),
             pltpu.VMEM((1, NY * ROWS), i32),
+            pltpu.VMEM((WIDTH, WIDTH), bf16),
             pltpu.VMEM((WIDTH, WIDTH), bf16),
             pltpu.VMEM((WIDTH, WIDTH), bf16),
             pltpu.VMEM((ROWS, WIDTH), bf16),
@@ -521,10 +545,10 @@
             pltpu.VMEM((piece, WIDTH), bf16),
             pltpu.VMEM((piece, WIDTH), bf16),
             pltpu.VMEM((2 * piece, WIDTH), f32),
-            pltpu.VMEM((NZ - 1, 2 * piece // NZ, WIDTH), f32),
-            pltpu.VMEM((NY, 2 * piece // NZ, WIDTH), f32),
-            pltpu.VMEM((2 * piece, WIDTH), f32),
-            pltpu.VMEM((NC, NX, 2 * piece, WIDTH), bf16),
+            pltpu.VMEM((NZ, 4 * piece // NZ, WIDTH // 2), bf16),
+            pltpu.VMEM((NZ - 1, 4 * piece // NZ, WIDTH // 2), bf16),
+            pltpu.VMEM((NY, 4 * piece // NZ, WIDTH // 2), bf16),
+            pltpu.VMEM((NC, NX, NZ, 4 * piece // NZ, WIDTH // 2), bf16),
             pltpu.VMEM((2, WIDTH, WIDTH), f32),
             pltpu.SemaphoreType.DMA((n_copies,)),
             pltpu.SemaphoreType.DMA((n_copies,)),

time: 100 us -> 99.3 us (level)
  no operation moved by 1% of the time
where the time goes in v6:
time: 99.3 us; the launch traced here: 99.1 us
  Pallas kernels  98.5 us (99%)
    pallas_call x1, Pallas kernels, per_device(): pl.pallas_call(kernel, out_shape=shapes, in_specs=[anywhere] * 10, out_sp...  96.6 us

profile of v6, /device:TPU:1, one launch (start us, length us, event | category | flops | bytes accessed | tf_op | source)
XLA Modules:
  0.0 99.1 jit_solution(15760380310802602411)
XLA Ops:
  0.6 96.6 %layers.1 = (bf16[128,256]{1,0:T(8,128)(2,1)}, bf16[128,256]{1,0:T(8,128)(2,1)}, f32[256,256]{1,0:T(8,128)}, f32[256,256]{1,0:T(8,128)}) custom-call(bf16[128,256]{1,0:T(8,128)(2,1)} %feat.1, bf16[128,256]{1,0:T(8,128)(2,1)} %hist.1, bf16[128,512]{1,0:T(8,128)(2,1)} %adj_in.1, bf16[64,4096]{1,0:T(8,128)(2,1)} %tiles_in.1, s32[1,1024]{1,0:T(1,128)} %target_in.1, ...), custom_call_target="tpu_custom_call" | custom-call | tf_op jit(solution)/shard_map/layers/pallas_call | solution.py:503
  97.2 1.9 %keep.1 = (bf16[128,256]{1,0:T(8,128)(2,1)}, bf16[128,256]{1,0:T(8,128)(2,1)}, f32[256,256]{1,0:T(8,128)}, f32[256,256]{1,0:T(8,128)}) custom-call(bf16[128,256]{1,0:T(8,128)(2,1)} %get-tuple-element.8.refs_0_, bf16[128,256]{1,0:T(8,128)(2,1)} %get-tuple-element.9.refs_1_, f32[256,256]{1,0:T(8,128)} %get-tuple-element.10.refs_2_, ...), custom_call_target="tpu_custom_call" | custom-call | tf_op jit(solution)/shard_map/keep/pallas_call | solution.py:562

commit v7 on v6

--- a/solution.py
+++ b/solution.py
@@ -76,11 +76,11 @@
 
 def kernel(
     feat, hist, adj_in, tiles_in, target_in, counts_in, sends_in, w1_in, w2_in, cot_in,
-    fresh_out, layer_out, grad1, grad2,
+    fresh_out, layer_out, final_out,
     adj, tiles, target, counts, sends, w1, w2, w2_t, cot, layer,
     held, sb, code, used, chosen, codes, edges, twin_edges, seen, blocks,
     for_twin, of_twin, parts, second_hop, relay3, relay4, got,
-    rows, slopes, turned, share, rounded, from_twin, halves, sending, from_row, leaving, arriving, part, folded, from_z, from_y, final, grads, send, recv, near,
+    rows, slopes, turned, share, rounded, from_twin, halves, sending, from_row, leaving, arriving, part, folded, from_z, from_y, final, send, recv, near,
 ):
     y, z, c, x = position()
     links = Links(send, recv)
@@ -456,32 +456,37 @@
         arrive([copy])
         crossings.append(push(final.at[c, (x + NX - k) % NX], twin))
 
-    def unpack(core):
-        for m in range(NX):
-            for k in range(NZ):
-                which, row = divmod(k * small, piece)
-                at = pl.ds(pl.multiple_of(core * half + m * piece + row, small), small)
-                value = final[core, m, k].astype(jnp.float32)
-                grads[which, at, 0:lanes] = value[:small]
-                grads[which, at, lanes:WIDTH] = value[small:]
-
-    unpack(c)
+    results.append(here(final.at[c], final_out.at[c]))
     arrive(crossings)
-    unpack(1 - c)
-    results += [here(grads.at[0], grad1), here(grads.at[1], grad2)]
+    results.append(here(final.at[1 - c], final_out.at[1 - c]))
     settle(0)
     for copy in results:
         copy.wait()
 
 
-def keep_kernel(*refs):
-    count = (len(refs) - 2) // 3
-    into, out = refs[-2:]
-    loads = [pltpu.make_async_copy(refs[k], refs[2 * count + k], into.at[k]) for k in range(count)]
-    stores = [pltpu.make_async_copy(refs[2 * count + k], refs[count + k], out.at[k]) for k in range(count)]
+def keep_kernel(
+    fresh_in, layer_in, final_in, fresh_out, layer_out, grad1, grad2, fresh, layer, final, grads, into, out
+):
+    pairs = ((final_in, final), (fresh_in, fresh), (layer_in, layer))
+    loads = [pltpu.make_async_copy(src, dst, into.at[k]) for k, (src, dst) in enumerate(pairs)]
+    pairs = ((grads.at[0], grad1), (grads.at[1], grad2), (fresh, fresh_out), (layer, layer_out))
+    stores = [pltpu.make_async_copy(src, dst, out.at[k]) for k, (src, dst) in enumerate(pairs)]
     for load in loads:
         load.start()
-    for load, store in zip(loads, stores):
+    half, lanes = WIDTH // NC, WIDTH // 2
+    piece = half // NX
+    small = 2 * piece // NZ
+    loads[0].wait()
+    for which in range(2):
+        for core in range(NC):
+            for m in range(NX):
+                for k in range(which * NZ // 2, (which + 1) * NZ // 2):
+                    row = core * half + m * piece + k * small - which * piece
+                    value = final[core, m, k].astype(jnp.float32)
+                    grads[which, row : row + small, 0:lanes] = value[:small]
+                    grads[which, row : row + small, lanes:WIDTH] = value[small:]
+        stores[which].start()
+    for load, store in zip(loads[1:], stores[2:]):
         load.wait()
         store.start()
     for store in stores:
@@ -500,11 +505,12 @@
         jax.ShapeDtypeStruct((WIDTH, WIDTH), f32),
         jax.ShapeDtypeStruct((WIDTH, WIDTH), f32),
     )
+    packed = jax.ShapeDtypeStruct((NC, NX, NZ, 4 * piece // NZ, WIDTH // 2), bf16)
     results = pl.pallas_call(
         kernel,
-        out_shape=shapes,
+        out_shape=shapes[:2] + (packed,),
         in_specs=[anywhere] * 10,
-        out_specs=(anywhere,) * 4,
+        out_specs=(anywhere,) * 3,
         scratch_shapes=[
             pltpu.VMEM((NX * ROWS, NX * ROWS), bf16),
             pltpu.VMEM((TILE, NY * span), bf16),
@@ -549,7 +555,6 @@
             pltpu.VMEM((NZ - 1, 4 * piece // NZ, WIDTH // 2), bf16),
             pltpu.VMEM((NY, 4 * piece // NZ, WIDTH // 2), bf16),
             pltpu.VMEM((NC, NX, NZ, 4 * piece // NZ, WIDTH // 2), bf16),
-            pltpu.VMEM((2, WIDTH, WIDTH), f32),
             pltpu.SemaphoreType.DMA((n_copies,)),
             pltpu.SemaphoreType.DMA((n_copies,)),
             pltpu.SemaphoreType.DMA((16,)),
@@ -562,10 +567,11 @@
     return pl.pallas_call(
         keep_kernel,
         out_shape=shapes,
-        in_specs=[anywhere] * 4,
+        in_specs=[anywhere] * 3,
         out_specs=(anywhere,) * 4,
-        scratch_shapes=[pltpu.VMEM(shape.shape, shape.dtype) for shape in shapes]
-        + [pltpu.SemaphoreType.DMA((4,)), pltpu.SemaphoreType.DMA((4,))],
+        scratch_shapes=[pltpu.VMEM(shape.shape, shape.dtype) for shape in shapes[:2] + (packed,)]
+        + [pltpu.VMEM((2, WIDTH, WIDTH), f32)]
+        + [pltpu.SemaphoreType.DMA((3,)), pltpu.SemaphoreType.DMA((4,))],
         compiler_params=pltpu.CompilerParams(vmem_limit_bytes=60 * 1024 * 1024),
         name="keep",
     )(*results)

time: 99.3 us -> 99.2 us (level)
  no operation moved by 1% of the time
where the time goes in v7:
time: 99.2 us; the launch traced here: 99 us
  Pallas kernels  98.4 us (99%)
    pallas_call x1, Pallas kernels, per_device(): pl.pallas_call(kernel, out_shape=shapes[:2] + (packed,), in_specs=[anywhe...  96.5 us

profile of v7, /device:TPU:1, one launch (start us, length us, event | category | flops | bytes accessed | tf_op | source)
XLA Modules:
  0.0 99.0 jit_solution(4717299955919989229)
XLA Ops:
  0.6 96.5 %layers.1 = (bf16[128,256]{1,0:T(8,128)(2,1)}, bf16[128,256]{1,0:T(8,128)(2,1)}, bf16[2,4,8,16,128]{4,3,2,1,0:T(8,128)(2,1)}) custom-call(bf16[128,256]{1,0:T(8,128)(2,1)} %feat.1, bf16[128,256]{1,0:T(8,128)(2,1)} %hist.1, bf16[128,512]{1,0:T(8,128)(2,1)} %adj_in.1, bf16[64,4096]{1,0:T(8,128)(2,1)} %tiles_in.1, s32[1,1024]{1,0:T(1,128)} %target_in.1, ...), custom_call_target="tpu_custom_call" | custom-call | tf_op jit(solution)/shard_map/layers/pallas_call | solution.py:509
  97.2 1.9 %keep.1 = (bf16[128,256]{1,0:T(8,128)(2,1)}, bf16[128,256]{1,0:T(8,128)(2,1)}, f32[256,256]{1,0:T(8,128)}, f32[256,256]{1,0:T(8,128)}) custom-call(bf16[128,256]{1,0:T(8,128)(2,1)} %get-tuple-element.7.fresh_in, bf16[128,256]{1,0:T(8,128)(2,1)} %get-tuple-element.8.layer_in, bf16[2,4,8,16,128]{4,3,2,1,0:T(8,128)(2,1)} %get-tuple-element.9.final_in), custom_call_target="tpu_custom_call" | custom-call | tf_op jit(solution)/shard_map/keep/pallas_call | solution.py:567
